TPU v7x, 32 devices: a whole 2x2x4 slice. The times are simulated.
32 devices in a mesh: fsdp: 8 (over z, x), rep: 4 (over y, core).
Axes of the slice: x: 2, y: 2, z: 4, core: 2. Of those that a mesh axis runs over, the one named last changes fastest.
Arguments:
- tokens: bfloat16 [24576, 960], P(('fsdp', 'rep')), may hold values from -6 to 6
- lengths: int32 [64, 3], P(('fsdp', 'rep')), may hold values from 1 to 288, 384 in all within a row
- attn_gain: bfloat16 [960], P('fsdp'), may hold values from 0.5 to 1.5
- w_query: bfloat16 [960, 960], P('fsdp', 'rep'), may hold values from -0.1875 to 0.1875
- w_key: bfloat16 [960, 320], P('fsdp', 'rep'), may hold values from -0.1875 to 0.1875
- w_value: bfloat16 [960, 320], P('fsdp', 'rep'), may hold values from -0.1875 to 0.1875
- w_output: bfloat16 [960, 960], P('fsdp', 'rep'), may hold values from -1.5 to 1.5
- mlp_gain: bfloat16 [960], P('fsdp'), may hold values from 0.5 to 1.5
- w_gate: bfloat16 [960, 2560], P('fsdp', 'rep'), may hold values from -0.1875 to 0.1875
- w_up: bfloat16 [960, 2560], P('fsdp', 'rep'), may hold values from -0.1875 to 0.1875
- w_down: bfloat16 [2560, 960], P('fsdp', 'rep'), may hold values from -0.125 to 0.125
- cotangent: bfloat16 [24576, 960], P(('fsdp', 'rep')), may hold values from -6 to 6
Outputs:
- output: bfloat16 [24576, 960], P(('fsdp', 'rep'))
- token_grad: bfloat16 [24576, 960], P(('fsdp', 'rep'))
- grad_attn_gain: float32 [960], P('fsdp')
- grad_query: float32 [960, 960], P('fsdp', 'rep')
- grad_key: float32 [960, 320], P('fsdp', 'rep')
- grad_value: float32 [960, 320], P('fsdp', 'rep')
- grad_output: float32 [960, 960], P('fsdp', 'rep')
- grad_mlp_gain: float32 [960], P('fsdp')
- grad_gate: float32 [960, 2560], P('fsdp', 'rep')
- grad_up: float32 [960, 2560], P('fsdp', 'rep')
- grad_down: float32 [2560, 960], P('fsdp', 'rep')
Inputs may be any that keep to these rules, and one draw needn't show every extreme that they name: Each row lists the lengths of the 3 sequences of one micro-batch; they sum to 384, and in every row the longest is exactly 288.
All inputs are finite; a program needn't handle non-finite values.
Results may differ from a plain program's by a relative error of at most 0.015.
Values may be sent and summed in bfloat16 or wider, within the bound.
No kernel may reach another device: no remote copies, remote signals or barrier semaphores. Data moves between devices by JAX's collectives and lax.ppermute only.
A program may use at most 192 MiB of HBM per device.

v0:
```python
import jax
import jax.numpy as jnp
from jax import lax
from jax.sharding import PartitionSpec as P

D = 960
HEADS = 15
KV_HEADS = 5
HEAD = 64
MB_TOK = 384
SEGS = 3
GROUP = 3
QW = 960
KVW = 320


norm_epsilon = 1e-05
rope_base = 100000.0
masked_value = -1e30


def layout(length_row):
    starts = jnp.cumsum(length_row) - length_row
    places = jnp.arange(MB_TOK, dtype=jnp.int32)
    inside = (
        (places[:, None] >= starts[None, :]) & (places[:, None] < (starts + length_row)[None, :])
    ).astype(jnp.int32)
    segment = jnp.sum(inside * jnp.arange(SEGS, dtype=jnp.int32)[None, :], axis=1)
    position = places - jnp.sum(inside * starts[None, :], axis=1)
    return (segment, position)


def visible(segment):
    places = jnp.arange(MB_TOK, dtype=jnp.int32)
    return (segment[:, None] == segment[None, :]) & (places[None, :] <= places[:, None])


def rope_tables(position):
    half_width = HEAD // 2
    exponent = jnp.arange(half_width, dtype=jnp.float32) * (2.0 / HEAD)
    inverse = jnp.power(rope_base, -exponent)
    angles = position.astype(jnp.float32)[..., None] * inverse
    return (jnp.cos(angles), jnp.sin(angles))


def rotate(values, cosine_table, sine_table, turning):
    half_width = values.shape[-1] // 2
    first_half = values[..., :half_width]
    second_half = values[..., half_width:]
    cosine_rows = cosine_table[..., None, :]
    sine_rows = sine_table[..., None, :] * turning
    return jnp.concatenate(
        [
            first_half * cosine_rows - second_half * sine_rows,
            second_half * cosine_rows + first_half * sine_rows,
        ],
        axis=-1,
    )


def norm_back(values, scale_rows, gain_row, upstream):
    weighted = upstream * gain_row
    gain_term = jnp.sum(upstream * values * scale_rows, axis=(0, 1))
    inner = jnp.mean(weighted * values, axis=-1, keepdims=True)
    return (
        scale_rows * weighted - values * scale_rows * scale_rows * scale_rows * inner,
        gain_term,
    )


def masked_scores(query_rot, key_rot, segment):
    scores = jnp.einsum(
        "qkgd,pkd->kgqp", query_rot, key_rot, preferred_element_type=jnp.float32
    ) * HEAD ** (-0.5)
    return jnp.where(visible(segment)[None, None], scores, masked_value)


def attend(items):
    query_rot, key_rot, value_rows, segment = items
    scores = masked_scores(query_rot, key_rot, segment)
    row_peak = jnp.max(scores, axis=-1, keepdims=True)
    log_total = row_peak + jnp.log(jnp.sum(jnp.exp(scores - row_peak), axis=-1, keepdims=True))
    probs_low = jnp.exp(scores - log_total).astype(jnp.bfloat16)
    mixed = jnp.einsum("kgqp,pkd->qkgd", probs_low, value_rows, preferred_element_type=jnp.float32)
    return (mixed.astype(jnp.bfloat16), log_total)


def attend_back(items):
    query_rot, key_rot, value_rows, segment, log_total, d_mixed = items
    probabilities = jnp.exp(masked_scores(query_rot, key_rot, segment) - log_total)
    probs_low = probabilities.astype(jnp.bfloat16)
    d_probs = jnp.einsum("qkgd,pkd->kgqp", d_mixed, value_rows, preferred_element_type=jnp.float32)
    d_scores = probabilities * (d_probs - jnp.sum(probabilities * d_probs, axis=-1, keepdims=True))
    d_scores = d_scores.astype(jnp.bfloat16)
    d_query_rot = jnp.einsum(
        "kgqp,pkd->qkgd", d_scores, key_rot, preferred_element_type=jnp.float32
    ) * HEAD ** (-0.5)
    d_key_rot = jnp.einsum(
        "kgqp,qkgd->pkd", d_scores, query_rot, preferred_element_type=jnp.float32
    ) * HEAD ** (-0.5)
    d_value = jnp.einsum("kgqp,qkgd->pkd", probs_low, d_mixed, preferred_element_type=jnp.float32)
    return (d_query_rot, d_key_rot, d_value)


def per_device(
    tokens,
    lengths,
    attn_gain,
    w_query,
    w_key,
    w_value,
    w_output,
    mlp_gain,
    w_gate,
    w_up,
    w_down,
    cotangent,
):
    f32 = jnp.float32
    bf16 = jnp.bfloat16
    widened = (
        lax.all_gather(w_query, "rep", axis=1, tiled=True),
        lax.all_gather(w_key, "rep", axis=1, tiled=True),
        lax.all_gather(w_value, "rep", axis=1, tiled=True),
        lax.all_gather(w_output, "rep", axis=1, tiled=True),
        lax.all_gather(w_gate, "rep", axis=1, tiled=True),
        lax.all_gather(w_up, "rep", axis=1, tiled=True),
        lax.all_gather(w_down, "rep", axis=1, tiled=True),
    )
    gathered = (
        lax.all_gather(widened[0], "fsdp", axis=0, tiled=True),
        lax.all_gather(widened[1], "fsdp", axis=0, tiled=True),
        lax.all_gather(widened[2], "fsdp", axis=0, tiled=True),
        lax.all_gather(widened[3], "fsdp", axis=0, tiled=True),
        lax.all_gather(widened[4], "fsdp", axis=0, tiled=True),
        lax.all_gather(widened[5], "fsdp", axis=0, tiled=True),
        lax.all_gather(widened[6], "fsdp", axis=0, tiled=True),
        lax.all_gather(attn_gain, "fsdp", axis=0, tiled=True),
        lax.all_gather(mlp_gain, "fsdp", axis=0, tiled=True),
    )
    mat_query, mat_key, mat_value, mat_output, mat_gate, mat_up, mat_down, gain_one, gain_two = (
        gathered
    )
    gain_one_f = gain_one.astype(f32)
    gain_two_f = gain_two.astype(f32)
    micro_count = tokens.shape[0] // MB_TOK
    segments, positions = jax.vmap(layout)(lengths)
    cosine_table, sine_table = rope_tables(positions)
    inputs = tokens.astype(f32).reshape(micro_count, MB_TOK, D)
    scale_one = lax.rsqrt(jnp.mean(inputs * inputs, axis=-1, keepdims=True) + norm_epsilon)
    normed = (inputs * scale_one * gain_one_f).astype(bf16)
    query_lin = jnp.dot(normed, mat_query, preferred_element_type=f32).reshape(
        micro_count, MB_TOK, HEADS, HEAD
    )
    key_lin = jnp.dot(normed, mat_key, preferred_element_type=f32).reshape(
        micro_count, MB_TOK, KV_HEADS, HEAD
    )
    query_rot = (
        rotate(query_lin, cosine_table, sine_table, 1.0)
        .astype(bf16)
        .reshape(micro_count, MB_TOK, KV_HEADS, GROUP, HEAD)
    )
    key_rot = rotate(key_lin, cosine_table, sine_table, 1.0).astype(bf16)
    value_rows = (
        jnp.dot(normed, mat_value, preferred_element_type=f32)
        .astype(bf16)
        .reshape(micro_count, MB_TOK, KV_HEADS, HEAD)
    )
    mixed, log_total = lax.map(attend, (query_rot, key_rot, value_rows, segments))
    mixed = mixed.reshape(micro_count, MB_TOK, QW)
    middle = inputs + jnp.dot(mixed, mat_output, preferred_element_type=f32)
    scale_two = lax.rsqrt(jnp.mean(middle * middle, axis=-1, keepdims=True) + norm_epsilon)
    normed_two = (middle * scale_two * gain_two_f).astype(bf16)
    gate_lin = jnp.dot(normed_two, mat_gate, preferred_element_type=f32)
    up_lin = jnp.dot(normed_two, mat_up, preferred_element_type=f32)
    gate_sigmoid = jax.nn.sigmoid(gate_lin)
    silu_gate = gate_lin * gate_sigmoid
    hidden = (silu_gate * up_lin).astype(bf16)
    final_sum = middle + jnp.dot(hidden, mat_down, preferred_element_type=f32)
    output = final_sum.astype(bf16).reshape(tokens.shape[0], D)
    widened_back = (
        lax.all_gather(w_query, "rep", axis=1, tiled=True),
        lax.all_gather(w_key, "rep", axis=1, tiled=True),
        lax.all_gather(w_value, "rep", axis=1, tiled=True),
        lax.all_gather(w_output, "rep", axis=1, tiled=True),
        lax.all_gather(w_gate, "rep", axis=1, tiled=True),
        lax.all_gather(w_up, "rep", axis=1, tiled=True),
        lax.all_gather(w_down, "rep", axis=1, tiled=True),
    )
    gathered_back = (
        lax.all_gather(widened_back[0], "fsdp", axis=0, tiled=True),
        lax.all_gather(widened_back[1], "fsdp", axis=0, tiled=True),
        lax.all_gather(widened_back[2], "fsdp", axis=0, tiled=True),
        lax.all_gather(widened_back[3], "fsdp", axis=0, tiled=True),
        lax.all_gather(widened_back[4], "fsdp", axis=0, tiled=True),
        lax.all_gather(widened_back[5], "fsdp", axis=0, tiled=True),
        lax.all_gather(widened_back[6], "fsdp", axis=0, tiled=True),
        lax.all_gather(attn_gain, "fsdp", axis=0, tiled=True),
        lax.all_gather(mlp_gain, "fsdp", axis=0, tiled=True),
    )
    mat_query, mat_key, mat_value, mat_output, mat_gate, mat_up, mat_down, gain_one, gain_two = (
        gathered_back
    )
    gain_one_f = gain_one.astype(f32)
    gain_two_f = gain_two.astype(f32)
    d_final_low = cotangent.reshape(micro_count, MB_TOK, D)
    d_final = d_final_low.astype(f32)
    grad_down = jnp.einsum("mlf,mld->fd", hidden, d_final_low, preferred_element_type=f32)
    d_hidden = jnp.einsum("mld,fd->mlf", d_final_low, mat_down, preferred_element_type=f32)
    d_gate = (d_hidden * up_lin * gate_sigmoid * (1.0 + gate_lin * (1.0 - gate_sigmoid))).astype(
        bf16
    )
    d_up = (d_hidden * silu_gate).astype(bf16)
    grad_gate = jnp.einsum("mld,mlf->df", normed_two, d_gate, preferred_element_type=f32)
    grad_up = jnp.einsum("mld,mlf->df", normed_two, d_up, preferred_element_type=f32)
    d_normed_two = jnp.einsum(
        "mlf,df->mld", d_gate, mat_gate, preferred_element_type=f32
    ) + jnp.einsum("mlf,df->mld", d_up, mat_up, preferred_element_type=f32)
    d_norm_two, grad_gain_two = norm_back(middle, scale_two, gain_two_f, d_normed_two)
    d_middle = d_final + d_norm_two
    d_branch = d_middle.astype(bf16)
    grad_output = jnp.einsum("mlc,mld->cd", mixed, d_branch, preferred_element_type=f32)
    d_mixed = jnp.einsum("mld,cd->mlc", d_branch, mat_output, preferred_element_type=f32).astype(
        bf16
    )
    d_mixed = d_mixed.reshape(micro_count, MB_TOK, KV_HEADS, GROUP, HEAD)
    d_query_rot, d_key_rot, d_value = lax.map(
        attend_back, (query_rot, key_rot, value_rows, segments, log_total, d_mixed)
    )
    d_query = (
        rotate(
            d_query_rot.reshape(micro_count, MB_TOK, HEADS, HEAD), cosine_table, sine_table, -1.0
        )
        .astype(bf16)
        .reshape(micro_count, MB_TOK, QW)
    )
    d_key = (
        rotate(d_key_rot, cosine_table, sine_table, -1.0)
        .astype(bf16)
        .reshape(micro_count, MB_TOK, KVW)
    )
    d_value = d_value.astype(bf16).reshape(micro_count, MB_TOK, KVW)
    grad_query = jnp.einsum("mld,mlc->dc", normed, d_query, preferred_element_type=f32)
    grad_key = jnp.einsum("mld,mlc->dc", normed, d_key, preferred_element_type=f32)
    grad_value = jnp.einsum("mld,mlc->dc", normed, d_value, preferred_element_type=f32)
    d_normed = jnp.einsum("mlc,dc->mld", d_query, mat_query, preferred_element_type=f32)
    d_normed = d_normed + jnp.einsum("mlc,dc->mld", d_key, mat_key, preferred_element_type=f32)
    d_normed = d_normed + jnp.einsum("mlc,dc->mld", d_value, mat_value, preferred_element_type=f32)
    d_norm_one, grad_gain_one = norm_back(inputs, scale_one, gain_one_f, d_normed)
    token_grad = (d_middle + d_norm_one).astype(bf16).reshape(tokens.shape[0], D)
    owned_sums = (
        lax.psum_scatter(grad_query, "fsdp", scatter_dimension=0, tiled=True),
        lax.psum_scatter(grad_key, "fsdp", scatter_dimension=0, tiled=True),
        lax.psum_scatter(grad_value, "fsdp", scatter_dimension=0, tiled=True),
        lax.psum_scatter(grad_output, "fsdp", scatter_dimension=0, tiled=True),
        lax.psum_scatter(grad_gate, "fsdp", scatter_dimension=0, tiled=True),
        lax.psum_scatter(grad_up, "fsdp", scatter_dimension=0, tiled=True),
        lax.psum_scatter(grad_down, "fsdp", scatter_dimension=0, tiled=True),
        lax.psum_scatter(grad_gain_one, "fsdp", scatter_dimension=0, tiled=True),
        lax.psum_scatter(grad_gain_two, "fsdp", scatter_dimension=0, tiled=True),
    )
    matrix_sums = (
        lax.psum_scatter(
            owned_sums[0].astype(jnp.bfloat16), "rep", scatter_dimension=1, tiled=True
        ).astype(jnp.float32),
        lax.psum_scatter(
            owned_sums[1].astype(jnp.bfloat16), "rep", scatter_dimension=1, tiled=True
        ).astype(jnp.float32),
        lax.psum_scatter(
            owned_sums[2].astype(jnp.bfloat16), "rep", scatter_dimension=1, tiled=True
        ).astype(jnp.float32),
        lax.psum_scatter(
            owned_sums[3].astype(jnp.bfloat16), "rep", scatter_dimension=1, tiled=True
        ).astype(jnp.float32),
        lax.psum_scatter(
            owned_sums[4].astype(jnp.bfloat16), "rep", scatter_dimension=1, tiled=True
        ).astype(jnp.float32),
        lax.psum_scatter(
            owned_sums[5].astype(jnp.bfloat16), "rep", scatter_dimension=1, tiled=True
        ).astype(jnp.float32),
        lax.psum_scatter(
            owned_sums[6].astype(jnp.bfloat16), "rep", scatter_dimension=1, tiled=True
        ).astype(jnp.float32),
    )
    gain_sums = lax.psum((owned_sums[7], owned_sums[8]), "rep")
    return (
        output,
        token_grad,
        gain_sums[0],
        matrix_sums[0],
        matrix_sums[1],
        matrix_sums[2],
        matrix_sums[3],
        gain_sums[1],
        matrix_sums[4],
        matrix_sums[5],
        matrix_sums[6],
    )


def solution(mesh):
    placed = (
        P(("fsdp", "rep"), None),
        P(("fsdp", "rep"), None),
        P("fsdp"),
        P("fsdp", "rep"),
        P("fsdp", "rep"),
        P("fsdp", "rep"),
        P("fsdp", "rep"),
        P("fsdp"),
        P("fsdp", "rep"),
        P("fsdp", "rep"),
        P("fsdp", "rep"),
        P(("fsdp", "rep"), None),
    )
    return jax.shard_map(
        per_device,
        mesh=mesh,
        in_specs=placed,
        out_specs=(
            P(("fsdp", "rep"), None),
            P(("fsdp", "rep"), None),
            P("fsdp"),
            P("fsdp", "rep"),
            P("fsdp", "rep"),
            P("fsdp", "rep"),
            P("fsdp", "rep"),
            P("fsdp"),
            P("fsdp", "rep"),
            P("fsdp", "rep"),
            P("fsdp", "rep"),
        ),
        check_vma=False,
    )
```

profile of v0, /device:TPU:0, one launch (start us, length us, event | category | flops | bytes accessed | tf_op | source)
XLA Modules:
  0.0 1341.1 jit_solution(31903211238488624)
XLA Ops:
  23.9 9.9 all_gather.76
  57.5 21.8 %all-reduce.8 = (bf16[960]{0:T(1024)(128)(2,1)S(1)}, bf16[960]{0:T(1024)(128)(2,1)S(1)}) all-reduce(bf16[960]{0:T(1024)(128)(2,1)S(1)} %dynamic-update-slice, bf16[960]{0:T(1024)(128)(2,1)S(1)} %dynamic-update-slice.1), channel_id=1, replica_groups=mesh['fsdp'=8,'rep'=4] {'fsdp'}, use_global_device_ids=true, to_apply=%add | all-reduce | flops 1920 | bytes 7680
  91.7 33.2 %all-gather.1 = bf16[8,120,320]{1,2,0:T(8,128)(2,1)S(1)} all-gather(bf16[1,120,320]{1,2,0:T(8,128)(2,1)S(1)} %bitcast.375), channel_id=1, replica_groups=mesh['fsdp'=8,'rep'=4] {'fsdp'}, dimensions={0}, use_global_device_ids=true | all-gather | bytes 691200 | tf_op jit(solution)/shard_map/all_gather | solution.py:132
  133.8 33.8 %all-gather = bf16[8,120,320]{1,2,0:T(8,128)(2,1)S(1)} all-gather(bf16[1,120,320]{1,2,0:T(8,128)(2,1)S(1)} %bitcast.376), channel_id=1, replica_groups=mesh['fsdp'=8,'rep'=4] {'fsdp'}, dimensions={0}, use_global_device_ids=true | all-gather | bytes 691200 | tf_op jit(solution)/shard_map/all_gather | solution.py:133
  185.0 15.7 %while.26 = (s32[]{:T(128)}, bf16[2,384,5,3,64]{1,4,3,2,0:T(8,128)(2,1)}, f32[2,5,3,384,1]{3,2,1,4,0:T(4,128)}, bf16[2,384,5,64]{1,3,2,0:T(8,128)(2,1)S(1)}, s32...) while((s32[]{:T(128)}, ...), condition=%wide.region_7.8_spmd, body=%wide.region_4.7_spmd.sunk | while | flops 591366528 | bytes 41101456 | solution.py:169
  212.9 10.3 fusion.68
  223.2 76.4 %all-gather.17.cloned.1.call-done = bf16[2560,960]{1,0:T(8,128)(2,1)} async-done(((bf16[320,960]{1,0:T(8,128)(2,1)}), bf16[2560,960]{1,0:T(8,128)(2,1)}) %all-gather.17.cloned.1.call-update) | async-done | bytes 4915216 | tf_op jit(solution)/shard_map/all_gather | solution.py:137
  299.6 9.0 fusion.62
  308.6 73.6 %all-gather.13.cloned.1.call-done = bf16[960,2560]{1,0:T(8,128)(2,1)} async-done(((bf16[120,2560]{1,0:T(8,128)(2,1)}), bf16[960,2560]{1,0:T(8,128)(2,1)}) %all-gather.13.cloned.1.call-update) | async-done | bytes 4915216 | tf_op jit(solution)/shard_map/all_gather | solution.py:135
  382.2 14.4 %multiply_convert_fusion.1 = (bf16[2,384,2560]{2,1,0:T(8,128)(2,1)S(1)}, bf16[2,384,2560]{2,1,0:T(8,128)(2,1)S(1)}, bf16[2,384,2560]{2,1,0:T(8,128)(2,1)}) fusion(f32[2,384,2560]{2,1,0:T(8,128)} %fusion.62, f32[2,384,2560]{2,1,0:T(8,128)} %fusion.68, bf16[2,384,960]{1,2,0:T(8,128)(2,1)} %multiply_convert_fusion.3, ...), kind=kOutput, calls=%fused_computation.72 | convolution fusion | flops 3804364800 | bytes 33914880 | tf_op jit(solution)/shard_map/dot_general | solution.py:174
  396.6 9.4 fusion.66
  421.4 27.6 %while.27 = (s32[]{:T(128)}, f32[2,384,5,3,64]{1,4,3,2,0:T(8,128)}, f32[2,384,5,64]{1,3,2,0:T(8,128)}, bf16[2,384,5,64]{1,3,2,0:T(8,128)(2,1)}, bf16[2,384,5,64]...) while((s32[]{:T(128)}, f32[2,384,5,3,64]{1,4,3,2,0:T(8,128)}, ...), condition=%wide.region_12.13_spmd, body=%wide.region_10.12_spmd.sunk | while | flops 1449683328 | bytes 106883368 | solution.py:227
  466.6 8.7 convolution_bitcast_fusion.2
  476.6 9.1 convolution_bitcast_fusion.1
  502.2 133.5 %all-reduce.10 = (f32[960]{0:T(1024)S(1)}, bf16[960,320]{0,1:T(8,128)(2,1)}, bf16[960,320]{0,1:T(8,128)(2,1)}, f32[960]{0:T(1024)S(1)}) all-reduce(f32[960]{0:T(1024)S(1)} %get-tuple-element.110, f32[960,320]{0,1:T(8,128)} %convolution_bitcast_fusion.7, ...), channel_id=2, replica_groups=mesh['fsdp'=8,'rep'=4] {'fsdp'}, use_global_device_ids=true, to_apply=%region_15.16.clone | all-reduce | flops 616320 | bytes 3701760
  646.8 168.2 %reduce-scatter.33.cloned.1.call-done = f32[120,2560]{1,0:T(8,128)} async-done(((f32[960,2560]{1,0:T(8,128)}), f32[120,2560]{1,0:T(8,128)}) %reduce-scatter.33.cloned.1.call-update) | async-done | bytes 1228816 | tf_op jit(solution)/shard_map/reduce_scatter | solution.py:256
  819.4 167.3 %reduce-scatter.35.cloned.1.call-done = f32[120,2560]{1,0:T(8,128)} async-done(((f32[960,2560]{1,0:T(8,128)}), f32[120,2560]{1,0:T(8,128)}) %reduce-scatter.35.cloned.1.call-update) | async-done | bytes 1228816 | tf_op jit(solution)/shard_map/reduce_scatter | solution.py:257
  991.4 175.8 %reduce-scatter.37.cloned.1.call-done = f32[320,960]{1,0:T(8,128)} async-done(((f32[2560,960]{1,0:T(8,128)}), f32[320,960]{1,0:T(8,128)}) %reduce-scatter.37.cloned.1.call-update) | async-done | bytes 1228816 | tf_op jit(solution)/shard_map/reduce_scatter | solution.py:258
  1192.8 18.4 %reduce-scatter.29.cloned.1.call-done = bf16[120,80]{0,1:T(8,128)(2,1)} async-done(((bf16[120,320]{0,1:T(8,128)(2,1)}), bf16[120,80]{0,1:T(8,128)(2,1)}) %reduce-scatter.29.cloned.1.call-update) | async-done | bytes 19216 | tf_op jit(solution)/shard_map/reduce_scatter | solution.py:269
  1212.6 21.6 %reduce-scatter.41.cloned.1.call-done = bf16[240,120]{1,0:T(8,128)(2,1)} async-done(((bf16[960,120]{1,0:T(8,128)(2,1)}), bf16[240,120]{1,0:T(8,128)(2,1)}) %reduce-scatter.41.cloned.1.call-update) | async-done | bytes 57616
  1235.8 21.4 %reduce-scatter.39.cloned.1.call-done = bf16[240,120]{1,0:T(8,128)(2,1)} async-done(((bf16[960,120]{1,0:T(8,128)(2,1)}), bf16[240,120]{1,0:T(8,128)(2,1)}) %reduce-scatter.39.cloned.1.call-update) | async-done | bytes 57616
  1258.8 23.3 %reduce-scatter.43.cloned.1.call-done = bf16[640,120]{1,0:T(8,128)(2,1)} async-done(((bf16[2560,120]{1,0:T(8,128)(2,1)}), bf16[640,120]{1,0:T(8,128)(2,1)}) %reduce-scatter.43.cloned.1.call-update) | async-done | bytes 153616
  1283.9 23.0 %reduce-scatter.45.cloned.1.call-done = bf16[640,120]{1,0:T(8,128)(2,1)} async-done(((bf16[2560,120]{1,0:T(8,128)(2,1)}), bf16[640,120]{1,0:T(8,128)(2,1)}) %reduce-scatter.45.cloned.1.call-update) | async-done | bytes 153616
  1308.8 23.6 %reduce-scatter.47.cloned.1.call-done = bf16[240,320]{1,0:T(8,128)(2,1)} async-done(((bf16[960,320]{1,0:T(8,128)(2,1)}), bf16[240,320]{1,0:T(8,128)(2,1)}) %reduce-scatter.47.cloned.1.call-update) | async-done | bytes 153616
  (298 shorter events, 238.4 us)
Async XLA Ops:
  7.2 169.8 %all-gather.9.cloned.1.call-start = ((), (), s32[]{:S(2)}) async-start(), calls=%async_computation.12 | async-start | bytes 2211840 | tf_op jit(solution)/shard_map/all_gather | solution.py:131
  16.2 184.5 %all-gather.11.cloned.1.call-start = ((), (), s32[]{:S(2)}) async-start(), calls=%async_computation.13 | async-start | bytes 2211840 | tf_op jit(solution)/shard_map/all_gather | solution.py:134
  23.8 189.1 %all-gather.15.cloned.1.call-start = ((), (), s32[]{:S(2)}) async-start(), calls=%async_computation.15 | async-start | bytes 5529600 | tf_op jit(solution)/shard_map/all_gather | solution.py:136
  33.8 265.8 %all-gather.17.cloned.1.call-start = ((), (), s32[]{:S(2)}) async-start(), calls=%async_computation.16 | async-start | bytes 5898240 | tf_op jit(solution)/shard_map/all_gather | solution.py:137
  43.9 338.2 %all-gather.13.cloned.1.call-start = ((), (), s32[]{:S(2)}) async-start(), calls=%async_computation.14 | async-start | bytes 5529600 | tf_op jit(solution)/shard_map/all_gather | solution.py:135
  52.2 587.0 %reduce-scatter.31.cloned.1.call-start = ((), (), s32[]{:S(2)}) async-start(), calls=%async_computation.20 | async-start | bytes 4423680 | tf_op jit(solution)/shard_map/reduce_scatter | solution.py:255
  55.1 119.8 %copy-start = (f32[768,960]{0,1:T(8,128)}, f32[768,960]{0,1:T(8,128)S(1)}, u32[]{:S(2)}) copy-start(f32[768,960]{0,1:T(8,128)S(1)} %convert_element_type.131) | copy-start | bytes 8847364
  79.2 95.6 %copy-start.33 = (f32[960]{0:T(1024)}, f32[960]{0:T(1024)S(1)}, u32[]{:S(2)}) copy-start(f32[960]{0:T(1024)S(1)} %convert_element_type.132) | copy-start | bytes 11524
  79.3 95.6 %copy-start.35 = (f32[2,384]{1,0:T(2,128)}, f32[2,384]{1,0:T(2,128)S(1)}, u32[]{:S(2)}) copy-start(f32[2,384]{1,0:T(2,128)S(1)} %rsqrt.21) | copy-start | bytes 9220
  82.2 46.4 %copy-start.38 = (bf16[120,80]{0,1:T(8,128)(2,1)S(1)}, bf16[120,80]{0,1:T(8,128)(2,1)}, u32[]{:S(2)}) copy-start(bf16[120,80]{0,1:T(8,128)(2,1)} %param.21) | copy-start | bytes 57604
  124.9 46.3 %copy-start.42 = (f32[32]{0:T(128)S(1)}, f32[32]{0:T(128)}, u32[]{:S(2)}) copy-start(f32[32]{0:T(128)} %negate_power_fusion) | copy-start | bytes 388
  208.7 90.9 %copy-start.17 = (bf16[768,960]{0,1:T(8,128)(2,1)S(1)}, bf16[768,960]{0,1:T(8,128)(2,1)}, u32[]{:S(2)}) copy-start(bf16[768,960]{0,1:T(8,128)(2,1)} %param.27) | copy-start | bytes 4423684
  417.2 227.6 %reduce-scatter.25.cloned.1.call-start = ((), (), s32[]{:S(2)}) async-start(), calls=%async_computation.17 | async-start | bytes 4423680 | tf_op jit(solution)/shard_map/reduce_scatter | solution.py:252
  421.4 27.6 %copy-start.15 = (f32[2,384,32]{1,2,0:T(8,128)S(1)}, f32[2,384,32]{1,2,0:T(8,128)}, u32[]{:S(2)}) copy-start(f32[2,384,32]{1,2,0:T(8,128)} %copy-done.14) | copy-start | bytes 294916
  456.5 358.5 %reduce-scatter.33.cloned.1.call-start = ((), (), s32[]{:S(2)}) async-start(), calls=%async_computation.21 | async-start | bytes 11059200 | tf_op jit(solution)/shard_map/reduce_scatter | solution.py:256
  466.5 520.2 %reduce-scatter.35.cloned.1.call-start = ((), (), s32[]{:S(2)}) async-start(), calls=%async_computation.22 | async-start | bytes 11059200 | tf_op jit(solution)/shard_map/reduce_scatter | solution.py:257
  475.3 691.9 %reduce-scatter.37.cloned.1.call-start = ((), (), s32[]{:S(2)}) async-start(), calls=%async_computation.23 | async-start | bytes 11796480 | tf_op jit(solution)/shard_map/reduce_scatter | solution.py:258
  485.7 705.7 %reduce-scatter.27.cloned.1.call-start = ((), (), s32[]{:S(2)}) async-start(), calls=%async_computation.18 | async-start | bytes 102400 | tf_op jit(solution)/shard_map/reduce_scatter | solution.py:266
  637.4 573.8 %reduce-scatter.29.cloned.1.call-start = ((), (), s32[]{:S(2)}) async-start(), calls=%async_computation.19 | async-start | bytes 102400 | tf_op jit(solution)/shard_map/reduce_scatter | solution.py:269
  639.2 595.1 %reduce-scatter.41.cloned.1.call-start = ((), (), s32[]{:S(2)}) async-start(), calls=%async_computation.25 | async-start | bytes 307200
  641.2 616.1 %reduce-scatter.39.cloned.1.call-start = ((), (), s32[]{:S(2)}) async-start(), calls=%async_computation.24 | async-start | bytes 307200
  646.7 635.4 %reduce-scatter.43.cloned.1.call-start = ((), (), s32[]{:S(2)}) async-start(), calls=%async_computation.26 | async-start | bytes 819200
  819.4 487.6 %reduce-scatter.45.cloned.1.call-start = ((), (), s32[]{:S(2)}) async-start(), calls=%async_computation.27 | async-start | bytes 819200
  991.1 341.3 %reduce-scatter.47.cloned.1.call-start = ((), (), s32[]{:S(2)}) async-start(), calls=%async_computation.28 | async-start | bytes 921600
  (55 other events, 248.3 us)
Sparse Core Ops, SparseCore 0:
  16.3 49.5 all-gather.8
  68.7 54.5 all-gather.10
  125.4 87.4 all-gather.14
  215.0 84.6 all-gather.16
  301.7 80.4 all-gather.12
  417.3 82.4 reduce-scatter.30
  504.0 140.7 reduce-scatter.24
  648.4 166.5 reduce-scatter.32
  818.6 168.0 reduce-scatter.34
  990.1 176.9 reduce-scatter.36
  1170.1 18.6 reduce-scatter.26
  1191.7 19.5 reduce-scatter.28
  1214.2 19.9 reduce-scatter.40
  1237.2 19.9 reduce-scatter.38
  1259.6 22.4 reduce-scatter.42
  1284.5 22.4 reduce-scatter.44
  1309.4 22.9 reduce-scatter.46
where the time goes:
time: 1350 us; the launch traced here: 1340 us
  waiting for transfers between devices  801 us (59%)
  blocking collectives  279 us (21%)
  matrix products  140 us (10%)
  local copies, waits for them, and re-layouts  59.6 us (4%)
  other arithmetic  43.4 us (3%)
  between operations  16.4 us (1%)
    reduce_scatter x1, waiting for transfers between devices, per_device(): lax.psum_scatter(grad_down, 'fsdp', scatter_dimension=0, tiled=True)  176 us
    reduce_scatter x1, waiting for transfers between devices, per_device(): lax.psum_scatter(grad_gate, 'fsdp', scatter_dimension=0, tiled=True)  168 us
    reduce_scatter x1, waiting for transfers between devices, per_device(): lax.psum_scatter(grad_up, 'fsdp', scatter_dimension=0, tiled=True)  167 us
    unnamed x2, blocking collectives  155 us
    unnamed x22, waiting for transfers between devices  113 us
    all_gather x1, waiting for transfers between devices, per_device(): lax.all_gather(widened[6], 'fsdp', axis=0, tiled=True)  76.4 us
    all_gather x1, waiting for transfers between devices, per_device(): lax.all_gather(widened[4], 'fsdp', axis=0, tiled=True)  73.6 us
    unnamed x115, local copies, waits for them, and re-layouts  35.8 us
  transfers between devices with their start and end apart: 17, of which 13 were waited for; matrix products, arithmetic and copies ran while one was open for 14% of the time, Pallas kernels for 0%

commit v1 on v0

v1 whole, which is shorter than its diff:
```python
import jax
import jax.numpy as jnp
from jax import lax
from jax.experimental import pallas as pl
from jax.experimental.pallas import tpu as pltpu
from jax.sharding import PartitionSpec as P

D = 960
FF = 2560
HEADS = 15
KV_HEADS = 5
HEAD = 64
MB_TOK = 384
SEGS = 3
GROUP = 3
QW = 960
KVW = 320

SLOTS = 8
REPS = 4
USED = 120
SLOT = 128
WIDE = SLOTS * SLOT
PACK = 640
HALF_PACK = 320
ROWS_A = 64
VMEM_BYTES = 60 * 1024 * 1024

norm_epsilon = 1e-05
rope_base = 100000.0
masked_value = -1e30

f32 = jnp.float32
bf16 = jnp.bfloat16


def layout(length_row):
    starts = jnp.cumsum(length_row) - length_row
    places = jnp.arange(MB_TOK, dtype=jnp.int32)
    inside = (
        (places[:, None] >= starts[None, :]) & (places[:, None] < (starts + length_row)[None, :])
    ).astype(jnp.int32)
    segment = jnp.sum(inside * jnp.arange(SEGS, dtype=jnp.int32)[None, :], axis=1)
    position = places - jnp.sum(inside * starts[None, :], axis=1)
    return (segment, position)


def rope_tables(position):
    half_width = HEAD // 2
    exponent = jnp.arange(half_width, dtype=f32) * (2.0 / HEAD)
    inverse = jnp.power(rope_base, -exponent)
    angles = position.astype(f32)[:, None] * inverse
    cosines, sines = (jnp.cos(angles), jnp.sin(angles))
    return (
        jnp.concatenate([cosines] * 4, axis=1),
        jnp.concatenate([-sines, sines, -sines, sines], axis=1),
    )


def slot_of(eighth):
    return (eighth & 1) * 4 + (eighth >> 1)


def eighth_of(slot):
    return (slot & 3) * 2 + (slot >> 2)


def feature_lanes(eighth_here):
    lanes = jnp.arange(WIDE, dtype=jnp.int32)
    eighth = eighth_of(lanes // SLOT) ^ eighth_here
    return jnp.where(lanes % SLOT < USED, eighth * USED + lanes % SLOT, -1)


def one_hot(rows, wanted):
    return (jnp.arange(rows, dtype=jnp.int32)[:, None] == wanted[None, :]).astype(bf16)


def placing(eighth_here, quarter_here):
    features = feature_lanes(eighth_here)
    spread = one_hot(WIDE, features)
    columns = jnp.arange(WIDE, dtype=jnp.int32)
    query_from = jnp.where(
        columns < QW, ((columns // 240) ^ quarter_here) * 256 + columns % 240, -1
    )
    key_columns = jnp.arange(384, dtype=jnp.int32)
    key_from = ((key_columns // 80) ^ quarter_here) * 384 + key_columns % 80
    key_value_from = jnp.concatenate(
        [
            jnp.where(key_columns < KVW, key_from + 112, -1),
            jnp.where(key_columns < KVW, key_from + 192, -1),
        ]
    )
    output_from = jnp.where(
        features >= 0, ((features // 240) ^ quarter_here) * 256 + 16 + features % 240, -1
    )
    return (
        spread,
        one_hot(1024, query_from),
        one_hot(1536, key_value_from),
        one_hot(1024, output_from),
    )


def dot_nn(left, right):
    return lax.dot_general(left, right, (((1,), (0,)), ((), ())), preferred_element_type=f32)


def dot_nt(left, right):
    return lax.dot_general(left, right, (((1,), (1,)), ((), ())), preferred_element_type=f32)


def dot_tn(left, right):
    return lax.dot_general(left, right, (((0,), (0,)), ((), ())), preferred_element_type=f32)


def lane_index(shape):
    return lax.broadcasted_iota(jnp.int32, shape, len(shape) - 1)


def swapped(values):
    first = (lane_index(values.shape) & 63) < 32
    return jnp.where(first, pltpu.roll(values, 96, 1), pltpu.roll(values, 32, 1))


def turned(values, cosines, sines):
    return values * cosines + swapped(values) * sines


def both_halves(values, odd):
    low = lane_index(values.shape) < 64
    moved = pltpu.roll(values, 64, 1)
    return jnp.where(low, moved, values) if odd else jnp.where(low, values, moved)


def only_half(values, odd):
    low = lane_index(values.shape) < 64
    return jnp.where(low != bool(odd), values, jnp.zeros_like(values))


def gain_row(attn_ref, which):
    rows = [attn_ref[0, s, 112:128, 0:SLOT].astype(f32)[8 + which : 9 + which] for s in range(SLOTS)]
    return jnp.concatenate(rows, axis=1)


def probs_at(part):
    return (0, 128, 384)[part]


def attn_forward_kernel(
    inputs,
    spread,
    query_from,
    key_value_from,
    output_from,
    cosines,
    sines,
    segment_rows,
    segment_columns,
    a0,
    a1,
    a2,
    a3,
    b0,
    b1,
    b2,
    b3,
    normed_out,
    query_out,
    key_out,
    value_out,
    probs_out,
    mixed_out,
    middle_out,
    normed_two_out,
    w_query,
    w_key_value,
    w_output,
    gains_out,
    attn_all,
    heads_out,
    mixed_heads,
    bias,
    sems,
):
    @pl.when(pl.program_id(0) == 0)
    def _():
        copies = []
        for quarter, source in enumerate((a0, a1, a2, a3)):
            copies.append((source, attn_all.at[quarter, :, 0:ROWS_A, :]))
        for place, source in enumerate((b0, b1, b2, b3)):
            side, core = (place >> 1, place & 1)
            for y in range(2):
                copies.append(
                    (
                        source.at[y * 4 : y * 4 + 4],
                        attn_all.at[y * 2 + core, side * 4 : side * 4 + 4, ROWS_A : 2 * ROWS_A, :],
                    )
                )
        started = [
            pltpu.make_async_copy(source, target, sems.at[n])
            for n, (source, target) in enumerate(copies)
        ]
        for copy in started:
            copy.start()
        for copy in started:
            copy.wait()

        def columns(low, high):
            return jnp.concatenate(
                [
                    attn_all[quarter, :, :, low:high].reshape(WIDE, high - low)
                    for quarter in range(REPS)
                ],
                axis=1,
            )

        w_query[...] = dot_nn(columns(0, 256), query_from[...]).astype(bf16)
        w_key_value[...] = dot_nn(columns(128, 512), key_value_from[...]).astype(bf16)
        w_output[...] = dot_nn(columns(384, 640), output_from[...]).astype(bf16)
        gains_out[0:1, :] = gain_row(attn_all, 0)
        gains_out[1:2, :] = gain_row(attn_all, 1)

    values = inputs[...].astype(f32)
    gain_one = gains_out[0:1, :]
    gain_two = gains_out[1:2, :]
    scale = lax.rsqrt(jnp.sum(values * values, axis=1, keepdims=True) * (1.0 / D) + norm_epsilon)
    normed = (values * scale * gain_one).astype(bf16)
    normed_out[...] = normed
    cosine, sine = (cosines[...], sines[...])
    query_lin = dot_nn(normed, w_query[...])
    for c in range(8):
        at = slice(c * 128, c * 128 + 128)
        query_out[:, at] = turned(query_lin[:, at], cosine, sine).astype(bf16)
    key_value = dot_nn(normed, w_key_value[...])
    for c in range(3):
        key_part = turned(key_value[:, c * 128 : c * 128 + 128], cosine, sine)
        value_part = key_value[:, 384 + c * 128 : 384 + c * 128 + 128]
        for odd in range(2 if c < 2 else 1):
            at = slice((2 * c + odd) * 128, (2 * c + odd) * 128 + 128)
            key_out[:, at] = both_halves(key_part, odd).astype(bf16)
            value_out[:, at] = both_halves(value_part, odd).astype(bf16)

    query_place = lax.broadcasted_iota(jnp.int32, (MB_TOK, MB_TOK), 0)
    key_place = lax.broadcasted_iota(jnp.int32, (MB_TOK, MB_TOK), 1)
    seen = (segment_rows[...] == segment_columns[0]) & (key_place <= query_place)
    bias[...] = jnp.where(seen, 0.0, masked_value)
    for j in range(KV_HEADS):
        at = slice(j * 128, j * 128 + 128)
        for part in range(3):
            keys = 128 * (part + 1)
            rows = slice(part * 128, part * 128 + 128)
            queries = jnp.concatenate(
                [
                    only_half(query_out[rows, (h // 2) * 128 : (h // 2) * 128 + 128], h % 2)
                    for h in range(3 * j, 3 * j + 3)
                ],
                axis=0,
            )
            scores = dot_nt(queries, key_out[0:keys, at]) * HEAD**-0.5
            hidden_part = bias[rows, 0:keys]
            scores = scores + jnp.concatenate([hidden_part] * GROUP, axis=0)
            peak = jnp.max(scores, axis=1, keepdims=True)
            weights = jnp.exp(scores - peak)
            total = jnp.sum(weights, axis=1, keepdims=True)
            probs = (weights * (1.0 / total)).astype(bf16)
            probs_out[0, j, :, probs_at(part) : probs_at(part) + keys] = probs
            gathered = dot_nn(probs, value_out[0:keys, at])
            for g in range(GROUP):
                heads_out[3 * j + g, rows, :] = gathered[g * 128 : g * 128 + 128]
    low = lane_index((MB_TOK, 128)) < 64
    for c in range(8):
        upper = heads_out[2 * c + 1] if 2 * c + 1 < HEADS else jnp.zeros((MB_TOK, 128), f32)
        mixed_heads[:, c * 128 : c * 128 + 128] = jnp.where(low, heads_out[2 * c], upper).astype(bf16)
    mixed = dot_nn(mixed_heads[...], spread[...]).astype(bf16)
    mixed_out[...] = mixed
    middle = values + dot_nn(mixed, w_output[...])
    middle_out[...] = middle
    scale_two = lax.rsqrt(
        jnp.sum(middle * middle, axis=1, keepdims=True) * (1.0 / D) + norm_epsilon
    )
    normed_two_out[...] = (middle * scale_two * gain_two).astype(bf16)


def whole_block(shape):
    return pl.BlockSpec(
        shape, lambda *ids: (0,) * len(shape), pipeline_mode=pl.Buffered(buffer_count=1)
    )


def anywhere():
    return pl.BlockSpec(memory_space=pl.ANY)


def attn_forward(inputs, places, tables, segments, first_parts, second_parts):
    tokens = inputs.shape[0]
    count = tokens // MB_TOK

    def per_batch(columns):
        return pl.BlockSpec((MB_TOK, columns), lambda i: (i, 0))

    outs = [
        jax.ShapeDtypeStruct((tokens, WIDE), bf16),
        jax.ShapeDtypeStruct((tokens, WIDE), bf16),
        jax.ShapeDtypeStruct((tokens, PACK), bf16),
        jax.ShapeDtypeStruct((tokens, PACK), bf16),
        jax.ShapeDtypeStruct((count, KV_HEADS, MB_TOK, 768), bf16),
        jax.ShapeDtypeStruct((tokens, WIDE), bf16),
        jax.ShapeDtypeStruct((tokens, WIDE), f32),
        jax.ShapeDtypeStruct((tokens, WIDE), bf16),
        jax.ShapeDtypeStruct((WIDE, 1024), bf16),
        jax.ShapeDtypeStruct((WIDE, 768), bf16),
        jax.ShapeDtypeStruct((WIDE, WIDE), bf16),
        jax.ShapeDtypeStruct((8, WIDE), f32),
    ]
    return pl.pallas_call(
        attn_forward_kernel,
        grid=(count,),
        in_specs=[per_batch(WIDE)]
        + [whole_block(place.shape) for place in places]
        + [
            per_batch(128),
            per_batch(128),
            per_batch(1),
            pl.BlockSpec((1, 1, MB_TOK), lambda i: (i, 0, 0)),
        ]
        + [anywhere()] * 8,
        out_specs=[
            per_batch(WIDE),
            per_batch(WIDE),
            per_batch(PACK),
            per_batch(PACK),
            pl.BlockSpec((1, KV_HEADS, MB_TOK, 768), lambda i: (i, 0, 0, 0)),
            per_batch(WIDE),
            per_batch(WIDE),
            per_batch(WIDE),
            whole_block((WIDE, 1024)),
            whole_block((WIDE, 768)),
            whole_block((WIDE, WIDE)),
            whole_block((8, WIDE)),
        ],
        out_shape=outs,
        scratch_shapes=[
            pltpu.VMEM((REPS, SLOTS, SLOT, PACK), bf16),
            pltpu.VMEM((HEADS, MB_TOK, 128), f32),
            pltpu.VMEM((MB_TOK, WIDE), bf16),
            pltpu.VMEM((MB_TOK, MB_TOK), f32),
            pltpu.SemaphoreType.DMA((12,)),
        ],
        compiler_params=pltpu.CompilerParams(vmem_limit_bytes=VMEM_BYTES),
        cost_estimate=pl.CostEstimate(
            flops=24_000_000_000, bytes_accessed=40_000_000, transcendentals=4_000_000
        ),
        name="attn_forward",
    )(
        inputs,
        *places,
        *tables,
        segments.reshape(tokens, 1),
        segments.reshape(count, 1, MB_TOK),
        *first_parts,
        *second_parts,
    )


def rolled(values):
    return pltpu.roll(values.astype(f32), HALF_PACK, 1)


def left_right(left, right):
    first = lane_index(left.shape) < HALF_PACK
    left, right = (left.astype(f32), right.astype(f32))
    return (
        jnp.where(first, left, pltpu.roll(right, HALF_PACK, 1)).astype(bf16),
        jnp.where(first, pltpu.roll(left, HALF_PACK, 1), right).astype(bf16),
    )


def mlp_kernel(
    here,
    normed,
    cotangent,
    cotangent_turned,
    g0,
    g1,
    g2,
    g3,
    d0,
    d1,
    d2,
    d3,
    out,
    d_normed,
    grads_zero,
    grads_one,
    down_zero,
    down_one,
    w_pair,
    down_raw,
    w_down,
    normed_turned,
    hidden_all,
    d_gate_all,
    d_up_all,
    grad_pair,
    grad_down,
    down_made,
    sem_pair,
    sem_down,
    sem_grad,
    sem_grad_down,
):
    step = pl.program_id(0)
    eighth_here, quarter_here = (here[0], here[1])
    side_here = eighth_here & 1
    slot = step & 1

    def pair_copies(at, to, core):
        return [
            pltpu.make_async_copy(
                (g0, g1, g2, g3)[side * 2 + core].at[pl.ds((at >> 1) * 4, 4)],
                w_pair.at[to, side * 4 : side * 4 + 4],
                sem_pair.at[to, side],
            )
            for side in range(2)
        ]

    def down_place(at, side):
        return side * 4 + ((at ^ quarter_here) ^ (eighth_here >> 1))

    def down_copies(at, to):
        return [
            pltpu.make_async_copy(
                (d0, d1, d2, d3)[quarter].at[down_place(at, side)],
                down_raw.at[to, side, quarter],
                sem_down.at[to, side, quarter],
            )
            for side in range(2)
            for quarter in range(REPS)
        ]

    def fetch(at, to):
        for core in range(2):

            @pl.when((at & 1) == core)
            def _():
                for copy in pair_copies(at, to, core):
                    copy.start()

        for copy in down_copies(at, to):
            copy.start()

    def grad_copies(at, to, core):
        return [
            pltpu.make_async_copy(
                grad_pair.at[to, side * 4 : side * 4 + 4],
                (grads_zero, grads_one)[core].at[side, pl.ds((at >> 1) * 4, 4)],
                sem_grad.at[to, side],
            )
            for side in range(2)
        ]

    def grad_down_copies(at, to):
        return [
            pltpu.make_async_copy(
                down_made.at[to, side, quarter],
                (down_zero, down_one)[quarter & 1].at[quarter >> 1, down_place(at, side)],
                sem_grad_down.at[to, side, quarter],
            )
            for side in range(2)
            for quarter in range(REPS)
        ]

    def settle(at, to):
        for copy in grad_copies(at, to, 0) + grad_down_copies(at, to):
            copy.wait()

    @pl.when(step == 0)
    def _():
        fetch(step, slot)
        normed_turned[...] = normed[...].T
        out[...] = jnp.zeros_like(out)
        d_normed[...] = jnp.zeros_like(d_normed)

    for copy in pair_copies(step, slot, 0) + down_copies(step, slot):
        copy.wait()

    @pl.when(step + 1 < REPS)
    def _():
        fetch(step + 1, 1 - slot)

    def rows_of(quarter, which):
        eighth = (quarter ^ quarter_here) * 2 + which
        return pl.multiple_of(slot_of(eighth ^ eighth_here) * SLOT, SLOT)

    for quarter in range(REPS):
        lefts, rights = left_right(
            down_raw[slot, side_here, quarter], down_raw[slot, 1 - side_here, quarter]
        )
        w_down[pl.ds(rows_of(quarter, 0), SLOT), :] = lefts
        w_down[pl.ds(rows_of(quarter, 1), SLOT), :] = rights

    tokens = normed.shape[0]
    w_gate = w_pair[slot, :, 0:SLOT, :].reshape(WIDE, PACK)
    w_up = w_pair[slot, :, SLOT : 2 * SLOT, :].reshape(WIDE, PACK)

    def one_tile(t, carry):
        rows = pl.ds(pl.multiple_of(t * 256, 256), 256)
        gate = dot_nn(normed[rows, :], w_gate)
        up = dot_nn(normed[rows, :], w_up)
        d_hidden = dot_nn(cotangent[rows, :], w_down[...])
        sigmoid = 1.0 / (1.0 + jnp.exp(-gate))
        silu = gate * sigmoid
        hidden = (silu * up).astype(bf16)
        d_gate = (d_hidden * up * sigmoid * (1.0 + gate * (1.0 - sigmoid))).astype(bf16)
        d_up = (d_hidden * silu).astype(bf16)
        hidden_all[rows, :] = hidden
        d_gate_all[rows, :] = d_gate
        d_up_all[rows, :] = d_up
        out[rows, :] += dot_nt(hidden, w_down[...])
        d_normed[rows, :] += dot_nt(d_gate, w_gate) + dot_nt(d_up, w_up)
        return carry

    lax.fori_loop(0, tokens // 256, one_tile, 0)

    @pl.when(step >= 2)
    def _():
        settle(step - 2, slot)

    def grad_tile(t, carry):
        rows = pl.ds(pl.multiple_of(t * 256, 256), 256)
        two = pl.ds(t * 2, 2)
        gate_part = dot_nn(normed_turned[rows, :], d_gate_all[...]).astype(bf16)
        grad_pair[slot, two, 0:SLOT, :] = gate_part.reshape(2, SLOT, PACK)
        up_part = dot_nn(normed_turned[rows, :], d_up_all[...]).astype(bf16)
        grad_pair[slot, two, SLOT : 2 * SLOT, :] = up_part.reshape(2, SLOT, PACK)
        grad_down[rows, :] = dot_nn(cotangent_turned[rows, :], hidden_all[...])
        return carry

    lax.fori_loop(0, WIDE // 256, grad_tile, 0)
    for quarter in range(REPS):
        lefts, rights = left_right(
            grad_down[pl.ds(rows_of(quarter, 0), SLOT), :],
            grad_down[pl.ds(rows_of(quarter, 1), SLOT), :],
        )
        down_made[slot, side_here, quarter] = lefts
        down_made[slot, 1 - side_here, quarter] = rights
    for core in range(2):

        @pl.when((step & 1) == core)
        def _():
            for copy in grad_copies(step, slot, core):
                copy.start()

    for copy in grad_down_copies(step, slot):
        copy.start()

    @pl.when(step == REPS - 1)
    def _():
        settle(step - 1, 1 - slot)
        settle(step, slot)


def mlp(here, normed, cotangent, cotangent_turned, pair_parts, down_parts):
    tokens = normed.shape[0]
    pair_grads = jax.ShapeDtypeStruct((2, SLOTS, 2 * SLOT, PACK), bf16)
    down_grads = jax.ShapeDtypeStruct((2, SLOTS, SLOT, PACK), bf16)
    return pl.pallas_call(
        mlp_kernel,
        grid=(REPS,),
        in_specs=[
            pl.BlockSpec(memory_space=pltpu.SMEM),
            whole_block((tokens, WIDE)),
            whole_block((tokens, WIDE)),
            whole_block((WIDE, tokens)),
        ]
        + [anywhere()] * 8,
        out_specs=[whole_block((tokens, WIDE)), whole_block((tokens, WIDE))] + [anywhere()] * 4,
        out_shape=[
            jax.ShapeDtypeStruct((tokens, WIDE), f32),
            jax.ShapeDtypeStruct((tokens, WIDE), f32),
            pair_grads,
            pair_grads,
            down_grads,
            down_grads,
        ],
        scratch_shapes=[
            pltpu.VMEM((2, SLOTS, 2 * SLOT, PACK), bf16),
            pltpu.VMEM((2, 2, REPS, SLOT, PACK), bf16),
            pltpu.VMEM((WIDE, PACK), bf16),
            pltpu.VMEM((WIDE, tokens), bf16),
            pltpu.VMEM((tokens, PACK), bf16),
            pltpu.VMEM((tokens, PACK), bf16),
            pltpu.VMEM((tokens, PACK), bf16),
            pltpu.VMEM((2, SLOTS, 2 * SLOT, PACK), bf16),
            pltpu.VMEM((WIDE, PACK), f32),
            pltpu.VMEM((2, 2, REPS, SLOT, PACK), bf16),
            pltpu.SemaphoreType.DMA((2, 2)),
            pltpu.SemaphoreType.DMA((2, 2, REPS)),
            pltpu.SemaphoreType.DMA((2, 2)),
            pltpu.SemaphoreType.DMA((2, 2, REPS)),
        ],
        compiler_params=pltpu.CompilerParams(vmem_limit_bytes=VMEM_BYTES),
        cost_estimate=pl.CostEstimate(
            flops=44_000_000_000, bytes_accessed=44_000_000, transcendentals=2_000_000
        ),
        name="mlp",
    )(here, normed, cotangent, cotangent_turned, *pair_parts, *down_parts)


def attn_backward_kernel(
    cotangent,
    middle,
    d_normed_two,
    inputs,
    query_rot,
    key_both,
    value_both,
    probs_in,
    cosines,
    sines,
    normed,
    mixed,
    gains,
    spread,
    query_from,
    key_value_from,
    output_from,
    w_query,
    w_key_value,
    w_output,
    token_grad,
    one_zero,
    one_one,
    two_zero,
    two_one,
    d_mixed_heads,
    head_parts,
    key_parts,
    value_parts,
    d_heads,
    wire_in,
    wire_out,
    gain_sums,
):
    step = pl.program_id(0)
    batches = pl.num_programs(0) - 1

    @pl.when(step < batches)
    def _():
        gain_one = gains[0:1, :]
        gain_two = gains[1:2, :]
        mid = middle[...]
        upstream = d_normed_two[...]
        scale_two = lax.rsqrt(jnp.sum(mid * mid, axis=1, keepdims=True) * (1.0 / D) + norm_epsilon)
        weighted = upstream * gain_two
        inner = jnp.sum(weighted * mid, axis=1, keepdims=True) * (1.0 / D)
        term_two = jnp.sum(upstream * mid * scale_two, axis=0, keepdims=True)
        d_middle = (
            cotangent[...].astype(f32)
            + scale_two * weighted
            - mid * scale_two * scale_two * scale_two * inner
        )
        d_branch = d_middle.astype(bf16)
        d_mixed = dot_nt(d_branch, w_output[...]).astype(bf16)
        d_mixed_heads[...] = dot_nt(d_mixed, spread[...]).astype(bf16)
        for j in range(KV_HEADS):
            at = slice(j * 128, j * 128 + 128)
            for part in (2, 1, 0):
                keys = 128 * (part + 1)
                rows = slice(part * 128, part * 128 + 128)

                def three(ref):
                    return jnp.concatenate(
                        [
                            only_half(ref[rows, (h // 2) * 128 : (h // 2) * 128 + 128], h % 2)
                            for h in range(3 * j, 3 * j + 3)
                        ],
                        axis=0,
                    )

                queries = three(query_rot)
                d_mix = three(d_mixed_heads)
                probs = probs_in[0, j, :, probs_at(part) : probs_at(part) + keys]
                probs_f = probs.astype(f32)
                d_probs = dot_nt(d_mix, value_both[0:keys, at])
                product = probs_f * d_probs
                d_scores = product - probs_f * jnp.sum(product, axis=1, keepdims=True)
                d_scores = d_scores.astype(bf16)
                d_query = dot_nn(d_scores, key_both[0:keys, at])
                for g in range(GROUP):
                    head_parts[3 * j + g, rows, :] = d_query[g * 128 : g * 128 + 128]
                d_key = dot_tn(d_scores, queries)
                d_value = dot_tn(probs, d_mix)
                if part == 2:
                    key_parts[j] = d_key
                    value_parts[j] = d_value
                else:
                    key_parts[j, 0:keys, :] += d_key
                    value_parts[j, 0:keys, :] += d_value

        low = lane_index((MB_TOK, 128)) < 64
        cosine, sine = (cosines[...], sines[...])
        empty = jnp.zeros((MB_TOK, 128), f32)
        for c in range(8):
            upper = head_parts[2 * c + 1] if 2 * c + 1 < HEADS else empty
            joined = jnp.where(low, head_parts[2 * c], upper) * HEAD**-0.5
            d_heads[:, c * 128 : c * 128 + 128] = turned(joined, cosine, -sine).astype(bf16)

        def summed(ref, j):
            return ref[j] + pltpu.roll(ref[j], 64, 1)

        for c in range(3):
            for place, ref in ((1024, key_parts), (1408, value_parts)):
                upper = summed(ref, 2 * c + 1) if 2 * c + 1 < KV_HEADS else empty
                joined = jnp.where(low, summed(ref, 2 * c), upper)
                if place == 1024:
                    joined = turned(joined * HEAD**-0.5, cosine, -sine)
                d_heads[:, place + c * 128 : place + c * 128 + 128] = joined.astype(bf16)
        d_query_low = d_heads[:, 0:1024]
        d_key_value_low = d_heads[:, 1024:1792]
        rows = pl.ds(pl.multiple_of(step * MB_TOK, MB_TOK), MB_TOK)
        query_wire = dot_nt(d_query_low, query_from[...])
        key_value_wire = dot_nt(d_key_value_low, key_value_from[...])
        output_wire = dot_nt(d_branch, output_from[...]).astype(bf16)
        for quarter in range(REPS):
            base = quarter * 512
            from_query = query_wire[:, quarter * 256 : quarter * 256 + 256]
            from_key = key_value_wire[:, quarter * 384 : quarter * 384 + 384]
            wire_in[rows, base : base + 128] = from_query[:, 0:128].astype(bf16)
            wire_in[rows, base + 128 : base + 256] = (
                from_query[:, 128:256] + from_key[:, 0:128]
            ).astype(bf16)
            wire_in[rows, base + 256 : base + 512] = from_key[:, 128:384].astype(bf16)
        wire_out[rows, :] = output_wire
        d_normed = dot_nt(d_query_low, w_query[...]) + dot_nt(d_key_value_low, w_key_value[...])
        values = inputs[...].astype(f32)
        scale = lax.rsqrt(
            jnp.sum(values * values, axis=1, keepdims=True) * (1.0 / D) + norm_epsilon
        )
        weighted = d_normed * gain_one
        inner = jnp.sum(weighted * values, axis=1, keepdims=True) * (1.0 / D)
        term_one = jnp.sum(d_normed * values * scale, axis=0, keepdims=True)
        total = d_middle + scale * weighted - values * scale * scale * scale * inner
        token_grad[...] = dot_nt(total.astype(bf16), spread[0:D, :]).astype(bf16)

        @pl.when(step == 0)
        def _():
            gain_sums[...] = jnp.zeros_like(gain_sums)

        gain_sums[0:1, :] += term_one
        gain_sums[1:2, :] += term_two

    @pl.when(step == batches)
    def _():
        normed_turned = normed[...].T
        mixed_turned = mixed[...].T
        row = lax.broadcasted_iota(jnp.int32, (SLOTS, 16, SLOT), 1)
        gain_rows = jnp.zeros((SLOTS, 16, SLOT), f32)
        for which in range(2):
            spots = [
                gain_sums[which : which + 1, s * SLOT : s * SLOT + SLOT].reshape(1, 1, SLOT)
                for s in range(SLOTS)
            ]
            gain_rows = jnp.where(row == 8 + which, jnp.concatenate(spots, axis=0), gain_rows)
        for quarter in range(REPS):
            first = dot_nn(normed_turned, wire_in[:, quarter * 512 : quarter * 512 + 512])
            second = dot_nn(mixed_turned, wire_out[:, quarter * 256 : quarter * 256 + 256])
            block = jnp.concatenate(
                [first[:, 0:384], first[:, 384:512] + second[:, 0:128], second[:, 128:256]], axis=1
            ).reshape(SLOTS, SLOT, PACK)
            y, core = (quarter >> 1, quarter & 1)
            low_rows = block[:, 0:ROWS_A, :].astype(bf16)
            high_rows = block[:, ROWS_A:SLOT, :].astype(bf16)
            (one_zero, one_one)[core][y, :, :, :] = low_rows
            target = (two_zero, two_one)[core]
            tail = (block[:, 112:SLOT, 0:SLOT] + gain_rows).astype(bf16)
            for side in range(2):
                slots = slice(side * 4, side * 4 + 4)
                target[side, y * 4 : y * 4 + 4, :, :] = high_rows[slots]
                target[side, y * 4 : y * 4 + 4, 48:64, 0:SLOT] = tail[slots]


def attn_backward(
    cotangent,
    middle,
    d_normed_two,
    inputs,
    query_rot,
    key_both,
    value_both,
    probs,
    tables,
    normed,
    mixed,
    gains,
    places,
    weights,
):
    tokens = inputs.shape[0]
    count = tokens // MB_TOK

    def per_batch(columns):
        return pl.BlockSpec((MB_TOK, columns), lambda i: (jnp.minimum(i, count - 1), 0))

    half = jax.ShapeDtypeStruct((2, SLOTS, ROWS_A, PACK), bf16)
    return pl.pallas_call(
        attn_backward_kernel,
        grid=(count + 1,),
        in_specs=[
            per_batch(WIDE),
            per_batch(WIDE),
            per_batch(WIDE),
            per_batch(WIDE),
            per_batch(WIDE),
            per_batch(PACK),
            per_batch(PACK),
            pl.BlockSpec(
                (1, KV_HEADS, MB_TOK, 768), lambda i: (jnp.minimum(i, count - 1), 0, 0, 0)
            ),
            per_batch(128),
            per_batch(128),
            whole_block((tokens, WIDE)),
            whole_block((tokens, WIDE)),
            whole_block((8, WIDE)),
        ]
        + [whole_block(place.shape) for place in places]
        + [whole_block(weight.shape) for weight in weights],
        out_specs=[per_batch(D)] + [whole_block(half.shape)] * 4,
        out_shape=[jax.ShapeDtypeStruct((tokens, D), bf16), half, half, half, half],
        scratch_shapes=[
            pltpu.VMEM((MB_TOK, WIDE), bf16),
            pltpu.VMEM((HEADS, MB_TOK, 128), f32),
            pltpu.VMEM((KV_HEADS, MB_TOK, 128), f32),
            pltpu.VMEM((KV_HEADS, MB_TOK, 128), f32),
            pltpu.VMEM((MB_TOK, 1792), bf16),
            pltpu.VMEM((tokens, REPS * 512), bf16),
            pltpu.VMEM((tokens, REPS * 256), bf16),
            pltpu.VMEM((8, WIDE), f32),
        ],
        compiler_params=pltpu.CompilerParams(vmem_limit_bytes=VMEM_BYTES),
        cost_estimate=pl.CostEstimate(
            flops=40_000_000_000, bytes_accessed=50_000_000, transcendentals=0
        ),
        name="attn_backward",
    )(
        cotangent,
        middle,
        d_normed_two,
        inputs,
        query_rot,
        key_both,
        value_both,
        probs,
        *tables,
        normed,
        mixed,
        gains,
        *places,
        *weights,
    )


Z_NEAR = ("fsdp", 1)
Z_FAR = ("fsdp", 2)
X_SIDE = ("fsdp", 0)
Y_SIDE = ("rep", 1)
CORE = ("rep", 0)


def swap_with(values, step):
    axis, bit = step
    count = lax.axis_size(axis)
    return lax.ppermute(values, axis, [(i, i ^ (1 << bit)) for i in range(count)])


def gather_parts(block, side_first):
    two = jnp.stack([block, swap_with(block, Z_NEAR)])
    four = jnp.concatenate([two, swap_with(two, Z_FAR)])
    first, second = (X_SIDE, Y_SIDE) if side_first else (Y_SIDE, X_SIDE)
    eight = jnp.concatenate([four, swap_with(four, first)])
    across = swap_with(eight, second)
    return (eight, swap_with(eight, CORE), across, swap_with(across, CORE))


def added(left, right):
    return (left.astype(f32) + right.astype(f32)).astype(bf16)


def scatter_parts(kept, sent, side_first):
    first, second = (X_SIDE, Y_SIDE) if side_first else (Y_SIDE, X_SIDE)
    came = swap_with(sent, CORE)
    came_next = swap_with(added(kept[1], came[1]), second)
    eight = added(kept[0], came[0])
    came = swap_with(added(eight[4:8], came_next[4:8]), first)
    four = added(eight[0:4], came_next[0:4])
    came_next = swap_with(added(four[2:4], came[2:4]), Z_FAR)
    two = added(four[0:2], came[0:2])
    came = swap_with(added(two[1], came_next[1]), Z_NEAR)
    return two[0].astype(f32) + came_next[0].astype(f32) + came.astype(f32)


def split_parts(blocks, side_first):
    rows, columns = blocks.shape[2:]
    grid = blocks.reshape(4, 2, 2, 2, rows, columns)
    parts = []
    for second in range(2):
        for core in range(2):
            if side_first:
                part = grid[:, :, second, core].transpose(1, 0, 2, 3)
            else:
                part = grid[:, second, :, core].transpose(1, 0, 2, 3)
            parts.append(part.reshape(SLOTS, rows, columns))
    return parts


def join_parts(kept, sent, side_first):
    rows, columns = kept.shape[2:]
    grid = jnp.stack([kept, sent]).reshape(2, 2, 2, 4, rows, columns)
    grid = grid.transpose(3, 2, 1, 0, 4, 5) if side_first else grid.transpose(3, 1, 2, 0, 4, 5)
    return grid.reshape(SLOTS, REPS, rows, columns)


def attn_block(w_query, w_key, w_value, w_output, attn_gain, mlp_gain):
    matrices = jnp.concatenate([w_query, w_key, w_value, w_output], axis=1)
    gains = jnp.stack([attn_gain, mlp_gain])
    gains = jnp.pad(gains, ((0, SLOT - USED - 2), (0, PACK - USED)))
    return jnp.concatenate([matrices, gains], axis=0)


def pair_block(w_gate, w_up):
    taller = ((0, SLOT - USED), (0, 0))
    return jnp.concatenate([jnp.pad(w_gate, taller), jnp.pad(w_up, taller)], axis=0)


def down_block(w_down):
    halves = w_down.T.reshape(2, USED, HALF_PACK)
    halves = jnp.concatenate([halves[0], halves[1]], axis=1)
    return jnp.pad(halves, ((0, SLOT - USED), (0, 0)))


def down_of(block):
    halves = jnp.stack([block[:USED, :HALF_PACK], block[:USED, HALF_PACK:]])
    return halves.reshape(2 * USED, HALF_PACK).T


def whole(shard):
    return lax.all_gather(lax.all_gather(shard, "rep", axis=1, tiled=True), "fsdp", axis=0, tiled=True)


def cut(matrix, eighth, quarter):
    rows, columns = (matrix.shape[0] // SLOTS, matrix.shape[1] // REPS)
    return matrix[
        eighth * rows : eighth * rows + rows, quarter * columns : quarter * columns + columns
    ]


def every_block(make):
    return jnp.stack(
        [jnp.stack([make(e, q) for q in range(REPS)]) for e in range(SLOTS)]
    )


def owned(blocks):
    eighths, quarters, rows, columns = blocks.shape
    matrix = blocks.transpose(0, 2, 1, 3).reshape(eighths * rows, quarters * columns)
    part = lax.psum_scatter(matrix, "fsdp", scatter_dimension=0, tiled=True)
    return lax.psum_scatter(part, "rep", scatter_dimension=1, tiled=True).astype(f32)


def per_device(
    tokens,
    lengths,
    attn_gain,
    w_query,
    w_key,
    w_value,
    w_output,
    mlp_gain,
    w_gate,
    w_up,
    w_down,
    cotangent,
):
    paired = lax.axis_size("fsdp") == SLOTS and lax.axis_size("rep") == REPS
    if paired:
        eighth_here = lax.axis_index("fsdp").astype(jnp.int32)
        quarter_here = lax.axis_index("rep").astype(jnp.int32)
        attn_pack = attn_block(w_query, w_key, w_value, w_output, attn_gain, mlp_gain)
        first_parts = gather_parts(attn_pack[:ROWS_A], True)
        second_parts = gather_parts(attn_pack[ROWS_A:], False)
        pair_parts = gather_parts(pair_block(w_gate, w_up), False)
        down_parts = gather_parts(down_block(w_down), True)
    else:
        eighth_here = jnp.int32(0)
        quarter_here = jnp.int32(0)
        gain_one, gain_two = (
            lax.all_gather(attn_gain, "fsdp", axis=0, tiled=True).reshape(SLOTS, USED),
            lax.all_gather(mlp_gain, "fsdp", axis=0, tiled=True).reshape(SLOTS, USED),
        )
        mats = [whole(w) for w in (w_query, w_key, w_value, w_output, w_gate, w_up, w_down)]
        attn_blocks = every_block(
            lambda e, q: attn_block(*[cut(m, e, q) for m in mats[:4]], gain_one[e], gain_two[e])
        )
        first_parts = split_parts(attn_blocks[:, :, :ROWS_A], True)
        second_parts = split_parts(attn_blocks[:, :, ROWS_A:], False)
        pair_parts = split_parts(
            every_block(lambda e, q: pair_block(cut(mats[4], e, q), cut(mats[5], e, q))), False
        )
        down_parts = split_parts(every_block(lambda e, q: down_block(cut(mats[6], e, q))), True)
    here = jnp.stack([eighth_here, quarter_here])
    places = placing(eighth_here, quarter_here)
    spread = places[0]
    segments, positions = jax.vmap(layout)(lengths)
    tables = rope_tables(positions.reshape(-1))
    inputs = jnp.dot(tokens, spread[:D], preferred_element_type=f32).astype(bf16)
    upstream = jnp.dot(cotangent, spread[:D], preferred_element_type=f32).astype(bf16)
    (
        normed,
        query_rot,
        key_both,
        value_both,
        probs,
        mixed,
        middle,
        normed_two,
        *weights,
        gains,
    ) = attn_forward(inputs, places, tables, segments, first_parts, second_parts)
    mlp_out, d_normed_two, pair_kept, pair_sent, down_kept, down_sent = mlp(
        here, normed_two, upstream, upstream.T, pair_parts, down_parts
    )
    output = jnp.dot(
        (middle + mlp_out).astype(bf16), spread[:D].T, preferred_element_type=f32
    ).astype(bf16)
    token_grad, one_kept, one_sent, two_kept, two_sent = attn_backward(
        upstream,
        middle,
        d_normed_two,
        inputs,
        query_rot,
        key_both,
        value_both,
        probs,
        tables,
        normed,
        mixed,
        gains,
        places,
        weights,
    )
    if paired:
        down_sum = scatter_parts(down_kept, down_sent, True)
        pair_sum = scatter_parts(pair_kept, pair_sent, False)
        first_sum = scatter_parts(one_kept, one_sent, True)
        second_sum = scatter_parts(two_kept, two_sent, False)
        attn_sum = jnp.concatenate([first_sum, second_sum], axis=0)
        gain_sums = (attn_sum[USED, :USED], attn_sum[USED + 1, :USED])
        attn_sum = attn_sum[:USED]
        grads = [
            attn_sum[:, 0:240],
            attn_sum[:, 240:320],
            attn_sum[:, 320:400],
            attn_sum[:, 400:640],
            pair_sum[:USED],
            pair_sum[SLOT : SLOT + USED],
            down_of(down_sum),
        ]
    else:
        attn_blocks = jnp.concatenate(
            [join_parts(one_kept, one_sent, True), join_parts(two_kept, two_sent, False)], axis=2
        )
        gain_sums = tuple(
            lax.psum(
                lax.psum_scatter(
                    attn_blocks[:, 0, USED + which, :USED].astype(f32).reshape(D),
                    "fsdp",
                    scatter_dimension=0,
                    tiled=True,
                ),
                "rep",
            )
            for which in range(2)
        )
        attn_blocks = attn_blocks[:, :, :USED]
        pair_blocks = join_parts(pair_kept, pair_sent, False)
        down_blocks = join_parts(down_kept, down_sent, True)
        grads = [
            owned(attn_blocks[..., 0:240]),
            owned(attn_blocks[..., 240:320]),
            owned(attn_blocks[..., 320:400]),
            owned(attn_blocks[..., 400:640]),
            owned(pair_blocks[:, :, :USED]),
            owned(pair_blocks[:, :, SLOT : SLOT + USED]),
            owned(jax.vmap(jax.vmap(down_of))(down_blocks)),
        ]
    return (
        output,
        token_grad,
        gain_sums[0],
        grads[0],
        grads[1],
        grads[2],
        grads[3],
        gain_sums[1],
        grads[4],
        grads[5],
        grads[6],
    )


def solution(mesh):
    placed = (
        P(("fsdp", "rep"), None),
        P(("fsdp", "rep"), None),
        P("fsdp"),
        P("fsdp", "rep"),
        P("fsdp", "rep"),
        P("fsdp", "rep"),
        P("fsdp", "rep"),
        P("fsdp"),
        P("fsdp", "rep"),
        P("fsdp", "rep"),
        P("fsdp", "rep"),
        P(("fsdp", "rep"), None),
    )
    return jax.shard_map(
        per_device,
        mesh=mesh,
        in_specs=placed,
        out_specs=(
            P(("fsdp", "rep"), None),
            P(("fsdp", "rep"), None),
            P("fsdp"),
            P("fsdp", "rep"),
            P("fsdp", "rep"),
            P("fsdp", "rep"),
            P("fsdp", "rep"),
            P("fsdp"),
            P("fsdp", "rep"),
            P("fsdp", "rep"),
            P("fsdp", "rep"),
        ),
        check_vma=False,
    )
```

time: 1350 us -> 514 us (0.38)
  waiting for transfers between devices: 801 us -> 240 us
  blocking collectives: 279 us -> 0 us
  Pallas kernels: 0 us -> 149 us
  matrix products: 140 us -> 10.9 us
  local copies, waits for them, and re-layouts: 59.6 us -> 14.3 us
  starting transfers between devices: 0.96 us -> 43.1 us
  between operations: 16.4 us -> 1.31 us
    reduce_scatter x7 -> x0, waiting for transfers between devices: 533 us -> none  [the longest x1 176 us: per_device(): lax.psum_scatter(grad_down, 'fsdp', scatter_dimension=0, tiled=True)]
    ppermute x0 -> x44, waiting for transfers between devices: none -> 240 us  [swap_with(): return lax.ppermute(values, axis, [(i, i ^ 1 << bit) for i in range(count)])]
    unnamed x2 -> x0, blocking collectives: 155 us -> none
    all_gather x5 -> x0, waiting for transfers between devices: 154 us -> none  [the longest x1 76.4 us: per_device(): lax.all_gather(widened[6], 'fsdp', axis=0, tiled=True)]
    pallas_call x0 -> x3, Pallas kernels: none -> 149 us  [the longest x1 65.5 us: mlp(): pl.pallas_call(mlp_kernel, grid=(REPS,), in_specs=[pl.BlockSpec(memory_sp...]
    dot_general x35 -> x3, matrix products: 140 us -> 10.9 us  [the longest x1 4.71 us: per_device(): jnp.dot(tokens, spread[:D], preferred_element_type=f32).astype(bf16)]
    all_gather x9 -> x0, blocking collectives: 117 us -> none  [the longest x1 33.8 us: per_device(): lax.all_gather(widened[2], 'fsdp', axis=0, tiled=True)]
    unnamed x22 -> x0, waiting for transfers between devices: 113 us -> none
  transfers between devices with their start and end apart: 17 -> 44, of which waited for: 13 -> 19; matrix products, arithmetic and copies ran while one was open for 14% -> 14% of each run, Pallas kernels for 0% -> 16%
where the time goes in v1:
time: 514 us; the launch traced here: 509 us
  waiting for transfers between devices  240 us (47%)
  Pallas kernels  149 us (29%)
  other arithmetic  50.9 us (10%)
  starting transfers between devices  43.1 us (8%)
  local copies, waits for them, and re-layouts  14.3 us (3%)
  matrix products  10.9 us (2%)
    ppermute x44, waiting for transfers between devices, swap_with(): return lax.ppermute(values, axis, [(i, i ^ 1 << bit) for i in range(count)])  240 us
    pallas_call x1, Pallas kernels, mlp(): pl.pallas_call(mlp_kernel, grid=(REPS,), in_specs=[pl.BlockSpec(memory_sp...  65.5 us
    pallas_call x1, Pallas kernels, attn_backward(): pl.pallas_call(attn_backward_kernel, grid=(count + 1,), in_specs=[per_bat...  48.6 us
    ppermute x44, starting transfers between devices, swap_with(): return lax.ppermute(values, axis, [(i, i ^ 1 << bit) for i in range(count)])  43.1 us
    pallas_call x1, Pallas kernels, attn_forward(): pl.pallas_call(attn_forward_kernel, grid=(count,), in_specs=[per_batch(WI...  34.8 us
    convert_element_type x16, other arithmetic, added(): return (left.astype(f32) + right.astype(f32)).astype(bf16)  19.5 us
  transfers between devices with their start and end apart: 44, of which 19 were waited for; matrix products, arithmetic and copies ran while one was open for 14% of the time, Pallas kernels for 16%

profile of v1, /device:TPU:0, one launch (start us, length us, event | category | flops | bytes accessed | tf_op | source)
XLA Modules:
  0.0 509.2 jit_solution(6939240455969989866)
XLA Ops:
  1.8 3.1 collective-permute-start.12
  14.4 3.1 collective-permute-start.13
  20.4 24.2 %collective-permute-done.13 = bf16[2,256,640]{2,1,0:T(8,128)(2,1)S(1)} collective-permute-done((bf16[2,256,640]{2,1,0:T(8,128)(2,1)}, bf16[2,256,640]{2,1,0:T(8,128)(2,1)S(1)}, u32[]{:S(2)}, u32[]{:S(2)}) %collective-permute-start.13) | collective-permute-done | bytes 655392 | tf_op jit(solution)/shard_map/ppermute | solution.py:873
  48.6 3.2 fusion.15
  54.3 19.5 %collective-permute-done.14 = bf16[4,256,640]{2,1,0:T(8,128)(2,1)S(1)} collective-permute-done((bf16[4,256,640]{2,1,0:T(8,128)(2,1)S(1)}, bf16[4,256,640]{2,1,0:T(8,128)(2,1)S(1)}, u32[]{:S(2)}, u32[]{:S(2)}) %collective-permute-start.14) | collective-permute-done | bytes 1310752 | tf_op jit(solution)/shard_map/ppermute | solution.py:873
  81.7 18.0 %collective-permute-done.1 = bf16[2,64,640]{2,1,0:T(8,128)(2,1)S(1)} collective-permute-done((bf16[2,64,640]{2,1,0:T(8,128)(2,1)S(1)}, bf16[2,64,640]{2,1,0:T(8,128)(2,1)S(1)}, u32[]{:S(2)}, u32[]{:S(2)}) %collective-permute-start.1) | collective-permute-done | bytes 163872 | tf_op jit(solution)/shard_map/ppermute | solution.py:873
  108.5 34.1 %collective-permute-done.2 = bf16[4,64,640]{2,1,0:T(8,128)(2,1)S(1)} collective-permute-done((bf16[4,64,640]{2,1,0:T(8,128)(2,1)S(1)}, bf16[4,64,640]{2,1,0:T(8,128)(2,1)S(1)}, u32[]{:S(2)}, u32[]{:S(2)}) %collective-permute-start.2) | collective-permute-done | bytes 327712 | tf_op jit(solution)/shard_map/ppermute | solution.py:873
  150.4 3.4 collective-permute-done.20
  161.6 4.7 fusion.21.inputs
  173.1 10.8 %collective-permute-done.22.d2 = bf16[8,128,640]{2,1,0:T(8,128)(2,1)} collective-permute-done((bf16[8,128,640]{2,1,0:T(8,128)(2,1)}, bf16[8,128,640]{2,1,0:T(8,128)(2,1)}, u32[]{:S(2)}, u32[]{:S(2)}) %collective-permute-start.22) | collective-permute-done | bytes 1310752 | tf_op jit(solution)/shard_map/ppermute | solution.py:873
  183.9 34.8 %attn_forward.1 = (bf16[768,1024]{1,0:T(8,128)(2,1)}, bf16[768,1024]{1,0:T(8,128)(2,1)}, bf16[768,640]{1,0:T(8,128)(2,1)}, bf16[768,640]{1,0:T(8,128)(2,1)}, bf1...) custom-call(bf16[768,1024]{1,0:T(8,128)(2,1)} %fusion.21.inputs, ...), custom_call_target="tpu_custom_call" | custom-call | flops 24000000000 | bytes 40000000 | tf_op jit(solution)/shard_map/attn_forward/pallas_call | solution.py:315
  220.3 65.5 %mlp.1 = (f32[768,1024]{1,0:T(8,128)}, f32[768,1024]{1,0:T(8,128)}, bf16[2,8,256,640]{3,2,1,0:T(8,128)(2,1)}, bf16[2,8,256,640]{3,2,1,0:T(8,128)(2,1)}, bf16[2,8...) custom-call(s32[2]{0:T(128)} %pad_add_fusion.1.here, bf16[768,1024]{1,0:T(8,128)(2,1)} %get-tuple-element.35.normed, ...), custom_call_target="tpu_custom_call" | custom-call | flops 44000002048 | bytes 44000000 | tf_op jit(solution)/shard_map/mlp/pallas_call | solution.py:567
  286.3 48.6 %attn_backward.1 = (bf16[768,960]{1,0:T(8,128)(2,1)}, bf16[2,8,64,640]{3,2,1,0:T(8,128)(2,1)}, bf16[2,8,64,640]{3,2,1,0:T(8,128)(2,1)}, bf16[2,8,64,640]{3,2,1,0:T(8,128)(2,1)}, bf16[2,8,64,640]{3,2,1,0:T(8,128)(2,1)}) custom-call(bf16[768,1024]{1,0:T(8,128)(2,1)} %bitcast.102, f32[768,1024]{1,0:T(8,128)} %get-tuple-element.34.middle, ...), custom_call_target="tpu_custom_call" | custom-call | flops 40000000000 | bytes 50000000 | tf_op jit(solution)/shard_map/attn_backward/pallas_call | solution.py:806
  340.6 5.8 %add_convert_fusion.1 = (bf16[1,8,256,640]{3,2,1,0:T(8,128)(2,1)S(1)}, bf16[8,256,640]{2,1,0:T(8,128)(2,1)}) fusion(bf16[2,8,256,640]{3,2,1,0:T(8,128)(2,1)} %collective-permute-done.34, bf16[2,8,256,640]{3,2,1,0:T(8,128)(2,1)} %get-tuple-element.53), kind=kLoop, calls=%fused_computation.1 | loop fusion | flops 10485760 | bytes 15728640 | tf_op jit(solution)/shard_map/convert_element_type | solution.py:886
  348.9 8.6 %collective-permute-done.25 = bf16[8,64,640]{2,1,0:T(8,128)(2,1)S(1)} collective-permute-done((bf16[8,64,640]{2,1,0:T(8,128)(2,1)S(1)}, bf16[8,64,640]{2,1,0:T(8,128)(2,1)S(1)}, u32[]{:S(2)}, u32[]{:S(2)}) %collective-permute-start.25) | collective-permute-done | bytes 655392 | tf_op jit(solution)/shard_map/ppermute | solution.py:873
  359.1 6.9 %collective-permute-done.30 = bf16[8,64,640]{2,1,0:T(8,128)(2,1)S(1)} collective-permute-done((bf16[8,64,640]{2,1,0:T(8,128)(2,1)S(1)}, bf16[8,64,640]{2,1,0:T(8,128)(2,1)S(1)}, u32[]{:S(2)}, u32[]{:S(2)}) %collective-permute-start.30) | collective-permute-done | bytes 655392 | tf_op jit(solution)/shard_map/ppermute | solution.py:873
  378.4 41.6 %collective-permute-done.31 = bf16[4,64,640]{2,1,0:T(8,128)(2,1)} collective-permute-done((bf16[4,64,640]{2,1,0:T(8,128)(2,1)}, bf16[4,64,640]{2,1,0:T(8,128)(2,1)}, u32[]{:S(2)}, u32[]{:S(2)}) %collective-permute-start.31) | collective-permute-done | bytes 327712 | tf_op jit(solution)/shard_map/ppermute | solution.py:873
  421.2 8.4 %collective-permute-start.28 = (bf16[64,640]{1,0:T(8,128)(2,1)S(1)}, bf16[64,640]{1,0:T(8,128)(2,1)S(1)}, u32[]{:S(2)}, u32[]{:S(2)}) collective-permute-start(bf16[64,640]{1,0:T(8,128)(2,1)S(1)} %fusion.44), channel_id=1, source_target_pairs={{0,8},{4,12},{8,0},{12,4},{16,24},{20,28},{24,16},{28,20},{1,9},{5... | collective-permute-start | bytes 245768 | tf_op jit(solution)/shard_map/ppermute | solution.py:873
  436.9 4.4 collective-permute-done.33
  441.3 9.0 %collective-permute-done.41 = bf16[4,128,640]{2,1,0:T(8,128)(2,1)S(1)} collective-permute-done((bf16[4,128,640]{2,1,0:T(8,128)(2,1)S(1)}, bf16[4,128,640]{2,1,0:T(8,128)(2,1)S(1)}, u32[]{:S(2)}, u32[]{:S(2)}) %collective-permute-start.41) | collective-permute-done | bytes 655392 | tf_op jit(solution)/shard_map/ppermute | solution.py:873
  451.5 10.2 %collective-permute-done.36 = bf16[4,256,640]{2,1,0:T(8,128)(2,1)S(1)} collective-permute-done((bf16[4,256,640]{2,1,0:T(8,128)(2,1)S(1)}, bf16[4,256,640]{2,1,0:T(8,128)(2,1)S(1)}, u32[]{:S(2)}, u32[]{:S(2)}) %collective-permute-start.36) | collective-permute-done | bytes 1310752 | tf_op jit(solution)/shard_map/ppermute | solution.py:873
  462.3 17.5 %collective-permute-done.42 = bf16[2,128,640]{2,1,0:T(8,128)(2,1)S(1)} collective-permute-done((bf16[2,128,640]{2,1,0:T(8,128)(2,1)S(1)}, bf16[2,128,640]{2,1,0:T(8,128)(2,1)S(1)}, u32[]{:S(2)}, u32[]{:S(2)}) %collective-permute-start.42) | collective-permute-done | bytes 327712 | tf_op jit(solution)/shard_map/ppermute | solution.py:873
  482.3 15.0 %collective-permute-done.43 = bf16[128,640]{1,0:T(8,128)(2,1)S(1)} collective-permute-done((bf16[128,640]{1,0:T(8,128)(2,1)S(1)}, bf16[128,640]{1,0:T(8,128)(2,1)S(1)}, u32[]{:S(2)}, u32[]{:S(2)}) %collective-permute-start.43) | collective-permute-done | bytes 163872 | tf_op jit(solution)/shard_map/ppermute | solution.py:873
  499.2 8.8 %collective-permute-done.38 = bf16[256,640]{1,0:T(8,128)(2,1)S(1)} collective-permute-done((bf16[256,640]{1,0:T(8,128)(2,1)}, bf16[256,640]{1,0:T(8,128)(2,1)S(1)}, u32[]{:S(2)}, u32[]{:S(2)}) %collective-permute-start.38) | collective-permute-done | bytes 327712 | tf_op jit(solution)/shard_map/ppermute | solution.py:873
  (180 shorter events, 98.6 us)
Async XLA Ops:
  8.2 72.5 %collective-permute-start.6 = (bf16[64,640]{1,0:T(8,128)(2,1)S(1)}, bf16[64,640]{1,0:T(8,128)(2,1)}, u32[]{:S(2)}, u32[]{:S(2)}) collective-permute-start(bf16[64,640]{1,0:T(8,128)(2,1)S(1)} %get-tuple-element.139), channel_id=1, source_target_pairs={{0,8},{4,12},{8,0},{12,4},{16,24},{20,28},{24,16},{28,20},{1,9},{5... | collective-permute-start | bytes 245768 | tf_op jit(solution)/shard_map/ppermute | solution.py:873
  8.3 68.4 %collective-permute-start = (bf16[64,640]{1,0:T(8,128)(2,1)S(1)}, bf16[64,640]{1,0:T(8,128)(2,1)}, u32[]{:S(2)}, u32[]{:S(2)}) collective-permute-start(bf16[64,640]{1,0:T(8,128)(2,1)S(1)} %get-tuple-element.140), channel_id=1, source_target_pairs={{0,8},{4,12},{8,0},{12,4},{16,24},{20,28},{24,16},{28,20},{1,9},{5... | collective-permute-start | bytes 245768 | tf_op jit(solution)/shard_map/ppermute | solution.py:873
  14.4 30.2 %collective-permute-start.13 = (bf16[2,256,640]{2,1,0:T(8,128)(2,1)}, bf16[2,256,640]{2,1,0:T(8,128)(2,1)S(1)}, u32[]{:S(2)}, u32[]{:S(2)}) collective-permute-start(bf16[2,256,640]{2,1,0:T(8,128)(2,1)} %pad_maximum_fusion.5), channel_id=1, source_target_pairs={{0,16},{4,20},{8,24},{12,28},{16,0},{20,4},{24,8},{28,12},{1,17},{... | collective-permute-start | bytes 1966088 | tf_op jit(solution)/shard_map/ppermute | solution.py:873
  18.2 59.5 %collective-permute-start.18 = (bf16[128,640]{1,0:T(8,128)(2,1)}, bf16[128,640]{1,0:T(8,128)(2,1)S(1)}, u32[]{:S(2)}, u32[]{:S(2)}) collective-permute-start(bf16[128,640]{1,0:T(8,128)(2,1)} %fusion.40), channel_id=1, source_target_pairs={{0,8},{4,12},{8,0},{12,4},{16,24},{20,28},{24,16},{28,20},{1,9},{5... | collective-permute-start | bytes 491528 | tf_op jit(solution)/shard_map/ppermute | solution.py:873
  44.8 29.0 %collective-permute-start.14 = (bf16[4,256,640]{2,1,0:T(8,128)(2,1)S(1)}, bf16[4,256,640]{2,1,0:T(8,128)(2,1)S(1)}, u32[]{:S(2)}, u32[]{:S(2)}) collective-permute-start(bf16[4,256,640]{2,1,0:T(8,128)(2,1)S(1)} %pad_maximum_fusion.1), channel_id=1, source_target_pairs={{0,2},{1,3},{2,0},{3,1},{4,6},{5,7},{6,4},{7,5},{8,10},{9,11},{10,... | collective-permute-start | bytes 3932168 | tf_op jit(solution)/shard_map/ppermute | solution.py:873
  75.6 94.2 %collective-permute-start.16 = (bf16[8,256,640]{2,1,0:T(8,128)(2,1)}, bf16[8,256,640]{2,1,0:T(8,128)(2,1)}, u32[]{:S(2)}, u32[]{:S(2)}) collective-permute-start(bf16[8,256,640]{2,1,0:T(8,128)(2,1)} %pad_maximum_fusion.g0), channel_id=1, source_target_pairs={{0,4},{4,0},{8,12},{12,8},{16,20},{20,16},{24,28},{28,24},{1,5},{5... | collective-permute-start | bytes 7864328 | tf_op jit(solution)/shard_map/ppermute | solution.py:873
  77.7 26.5 %collective-permute-start.19 = (bf16[2,128,640]{2,1,0:T(8,128)(2,1)S(1)}, bf16[2,128,640]{2,1,0:T(8,128)(2,1)S(1)}, u32[]{:S(2)}, u32[]{:S(2)}) collective-permute-start(bf16[2,128,640]{2,1,0:T(8,128)(2,1)S(1)} %pad_maximum_fusion.12), channel_id=1, source_target_pairs={{0,16},{4,20},{8,24},{12,28},{16,0},{20,4},{24,8},{28,12},{1,17},{... | collective-permute-start | bytes 983048 | tf_op jit(solution)/shard_map/ppermute | solution.py:873
  100.6 42.0 %collective-permute-start.2 = (bf16[4,64,640]{2,1,0:T(8,128)(2,1)S(1)}, bf16[4,64,640]{2,1,0:T(8,128)(2,1)S(1)}, u32[]{:S(2)}, u32[]{:S(2)}) collective-permute-start(bf16[4,64,640]{2,1,0:T(8,128)(2,1)S(1)} %pad_maximum_fusion.10), channel_id=1, source_target_pairs={{0,4},{4,0},{8,12},{12,8},{16,20},{20,16},{24,28},{28,24},{1,5},{5... | collective-permute-start | bytes 983048 | tf_op jit(solution)/shard_map/ppermute | solution.py:873
  105.2 48.6 %collective-permute-start.20 = (bf16[4,128,640]{2,1,0:T(8,128)(2,1)}, bf16[4,128,640]{2,1,0:T(8,128)(2,1)}, u32[]{:S(2)}, u32[]{:S(2)}) collective-permute-start(bf16[4,128,640]{2,1,0:T(8,128)(2,1)} %pad_maximum_fusion.6), channel_id=1, source_target_pairs={{0,4},{4,0},{8,12},{12,8},{16,20},{20,16},{24,28},{28,24},{1,5},{5... | collective-permute-start | bytes 1966088 | tf_op jit(solution)/shard_map/ppermute | solution.py:873
  107.4 39.7 %collective-permute-start.8 = (bf16[4,64,640]{2,1,0:T(8,128)(2,1)S(1)}, bf16[4,64,640]{2,1,0:T(8,128)(2,1)S(1)}, u32[]{:S(2)}, u32[]{:S(2)}) collective-permute-start(bf16[4,64,640]{2,1,0:T(8,128)(2,1)S(1)} %pad_maximum_fusion.11), channel_id=1, source_target_pairs={{0,2},{1,3},{2,0},{3,1},{4,6},{5,7},{6,4},{7,5},{8,10},{9,11},{10,... | collective-permute-start | bytes 983048 | tf_op jit(solution)/shard_map/ppermute | solution.py:873
  156.1 27.8 %collective-permute-start.22 = (bf16[8,128,640]{2,1,0:T(8,128)(2,1)}, bf16[8,128,640]{2,1,0:T(8,128)(2,1)}, u32[]{:S(2)}, u32[]{:S(2)}) collective-permute-start(bf16[8,128,640]{2,1,0:T(8,128)(2,1)} %pad_maximum_fusion.2.d0), channel_id=1, source_target_pairs={{0,2},{1,3},{2,0},{3,1},{4,6},{5,7},{6,4},{7,5},{8,10},{9,11},{10,... | collective-permute-start | bytes 3932168 | tf_op jit(solution)/shard_map/ppermute | solution.py:873
  169.3 49.5 %collective-permute-start.15 = (bf16[8,256,640]{2,1,0:T(8,128)(2,1)}, bf16[8,256,640]{2,1,0:T(8,128)(2,1)}, u32[]{:S(2)}, u32[]{:S(2)}) collective-permute-start(bf16[8,256,640]{2,1,0:T(8,128)(2,1)} %pad_maximum_fusion.g0), channel_id=1, source_target_pairs={{0,1},{1,0},{2,3},{3,2},{4,5},{5,4},{6,7},{7,6},{8,9},{9,8},{10,11... | collective-permute-start | bytes 7864328 | tf_op jit(solution)/shard_map/ppermute | solution.py:873
  169.8 49.0 %collective-permute-start.17 = (bf16[8,256,640]{2,1,0:T(8,128)(2,1)}, bf16[8,256,640]{2,1,0:T(8,128)(2,1)}, u32[]{:S(2)}, u32[]{:S(2)}) collective-permute-start(bf16[8,256,640]{2,1,0:T(8,128)(2,1)} %collective-permute-done.16.g2), channel_id=1, source_target_pairs={{0,1},{1,0},{2,3},{3,2},{4,5},{5,4},{6,7},{7,6},{8,9},{9,8},{10,11... | collective-permute-start | bytes 7864328 | tf_op jit(solution)/shard_map/ppermute | solution.py:873
  172.7 46.1 %collective-permute-start.21 = (bf16[8,128,640]{2,1,0:T(8,128)(2,1)}, bf16[8,128,640]{2,1,0:T(8,128)(2,1)S(1)}, u32[]{:S(2)}, u32[]{:S(2)}) collective-permute-start(bf16[8,128,640]{2,1,0:T(8,128)(2,1)} %pad_maximum_fusion.2.d0), channel_id=1, source_target_pairs={{0,1},{1,0},{2,3},{3,2},{4,5},{5,4},{6,7},{7,6},{8,9},{9,8},{10,11... | collective-permute-start | bytes 3932168 | tf_op jit(solution)/shard_map/ppermute | solution.py:873
  183.9 34.9 %collective-permute-start.23 = (bf16[8,128,640]{2,1,0:T(8,128)(2,1)}, bf16[8,128,640]{2,1,0:T(8,128)(2,1)S(1)}, u32[]{:S(2)}, u32[]{:S(2)}) collective-permute-start(bf16[8,128,640]{2,1,0:T(8,128)(2,1)} %collective-permute-done.22.d2), channel_id=1, source_target_pairs={{0,1},{1,0},{2,3},{3,2},{4,5},{5,4},{6,7},{7,6},{8,9},{9,8},{10,11... | collective-permute-start | bytes 3932168 | tf_op jit(solution)/shard_map/ppermute | solution.py:873
  285.8 54.8 %collective-permute-start.34 = (bf16[2,8,256,640]{3,2,1,0:T(8,128)(2,1)}, bf16[2,8,256,640]{3,2,1,0:T(8,128)(2,1)}, u32[]{:S(2)}, u32[]{:S(2)}) collective-permute-start(bf16[2,8,256,640]{3,2,1,0:T(8,128)(2,1)} %get-tuple-element.54), channel_id=1, source_target_pairs={{0,1},{1,0},{2,3},{3,2},{4,5},{5,4},{6,7},{7,6},{8,9},{9,8},{10,11... | collective-permute-start | bytes 15728648 | tf_op jit(solution)/shard_map/ppermute | solution.py:873
  335.0 32.5 %collective-permute-start.39 = (bf16[2,8,128,640]{3,2,1,0:T(8,128)(2,1)}, bf16[2,8,128,640]{3,2,1,0:T(8,128)(2,1)S(1)}, u32[]{:S(2)}, u32[]{:S(2)}) collective-permute-start(bf16[2,8,128,640]{3,2,1,0:T(8,128)(2,1)} %get-tuple-element.56), channel_id=1, source_target_pairs={{0,1},{1,0},{2,3},{3,2},{4,5},{5,4},{6,7},{7,6},{8,9},{9,8},{10,11... | collective-permute-start | bytes 7864328 | tf_op jit(solution)/shard_map/ppermute | solution.py:873
  346.4 83.2 %collective-permute-start.35 = (bf16[8,256,640]{2,1,0:T(8,128)(2,1)}, bf16[8,256,640]{2,1,0:T(8,128)(2,1)}, u32[]{:S(2)}, u32[]{:S(2)}) collective-permute-start(bf16[8,256,640]{2,1,0:T(8,128)(2,1)} %get-tuple-element.104), channel_id=1, source_target_pairs={{0,4},{4,0},{8,12},{12,8},{16,20},{20,16},{24,28},{28,24},{1,5},{5... | collective-permute-start | bytes 7864328 | tf_op jit(solution)/shard_map/ppermute | solution.py:873
  366.8 53.2 %collective-permute-start.31 = (bf16[4,64,640]{2,1,0:T(8,128)(2,1)}, bf16[4,64,640]{2,1,0:T(8,128)(2,1)}, u32[]{:S(2)}, u32[]{:S(2)}) collective-permute-start(bf16[4,64,640]{2,1,0:T(8,128)(2,1)} %get-tuple-element.120), channel_id=1, source_target_pairs={{0,4},{4,0},{8,12},{12,8},{16,20},{20,16},{24,28},{28,24},{1,5},{5... | collective-permute-start | bytes 983048 | tf_op jit(solution)/shard_map/ppermute | solution.py:873
  369.8 63.8 %collective-permute-start.40 = (bf16[8,128,640]{2,1,0:T(8,128)(2,1)}, bf16[8,128,640]{2,1,0:T(8,128)(2,1)}, u32[]{:S(2)}, u32[]{:S(2)}) collective-permute-start(bf16[8,128,640]{2,1,0:T(8,128)(2,1)} %get-tuple-element.106), channel_id=1, source_target_pairs={{0,2},{1,3},{2,0},{3,1},{4,6},{5,7},{6,4},{7,5},{8,10},{9,11},{10,... | collective-permute-start | bytes 3932168 | tf_op jit(solution)/shard_map/ppermute | solution.py:873
  378.3 42.9 %collective-permute-start.27 = (bf16[2,64,640]{2,1,0:T(8,128)(2,1)S(1)}, bf16[2,64,640]{2,1,0:T(8,128)(2,1)S(1)}, u32[]{:S(2)}, u32[]{:S(2)}) collective-permute-start(bf16[2,64,640]{2,1,0:T(8,128)(2,1)S(1)} %get-tuple-element.128), channel_id=1, source_target_pairs={{0,16},{4,20},{8,24},{12,28},{16,0},{20,4},{24,8},{28,12},{1,17},{... | collective-permute-start | bytes 491528 | tf_op jit(solution)/shard_map/ppermute | solution.py:873
  432.1 29.5 %collective-permute-start.36 = (bf16[4,256,640]{2,1,0:T(8,128)(2,1)S(1)}, bf16[4,256,640]{2,1,0:T(8,128)(2,1)S(1)}, u32[]{:S(2)}, u32[]{:S(2)}) collective-permute-start(bf16[4,256,640]{2,1,0:T(8,128)(2,1)S(1)} %get-tuple-element.108), channel_id=1, source_target_pairs={{0,2},{1,3},{2,0},{3,1},{4,6},{5,7},{6,4},{7,5},{8,10},{9,11},{10,... | collective-permute-start | bytes 3932168 | tf_op jit(solution)/shard_map/ppermute | solution.py:873
  450.6 29.3 %collective-permute-start.42 = (bf16[2,128,640]{2,1,0:T(8,128)(2,1)S(1)}, bf16[2,128,640]{2,1,0:T(8,128)(2,1)S(1)}, u32[]{:S(2)}, u32[]{:S(2)}) collective-permute-start(bf16[2,128,640]{2,1,0:T(8,128)(2,1)S(1)} %get-tuple-element.118), channel_id=1, source_target_pairs={{0,16},{4,20},{8,24},{12,28},{16,0},{20,4},{24,8},{28,12},{1,17},{... | collective-permute-start | bytes 983048 | tf_op jit(solution)/shard_map/ppermute | solution.py:873
  462.0 35.4 %collective-permute-start.37 = (bf16[2,256,640]{2,1,0:T(8,128)(2,1)S(1)}, bf16[2,256,640]{2,1,0:T(8,128)(2,1)S(1)}, u32[]{:S(2)}, u32[]{:S(2)}) collective-permute-start(bf16[2,256,640]{2,1,0:T(8,128)(2,1)S(1)} %get-tuple-element.112), channel_id=1, source_target_pairs={{0,16},{4,20},{8,24},{12,28},{16,0},{20,4},{24,8},{28,12},{1,17},{... | collective-permute-start | bytes 1966088 | tf_op jit(solution)/shard_map/ppermute | solution.py:873
  (38 other events, 492.8 us)

commit v2 on v1

--- a/solution.py
+++ b/solution.py
@@ -362,10 +362,6 @@
     )
 
 
-def rolled(values):
-    return pltpu.roll(values.astype(f32), HALF_PACK, 1)
-
-
 def left_right(left, right):
     first = lane_index(left.shape) < HALF_PACK
     left, right = (left.astype(f32), right.astype(f32))
@@ -375,236 +371,396 @@
     )
 
 
-def mlp_kernel(
+def pair_fetches(first_parts, second_parts, at, w_gate, w_up, sems):
+    found = []
+    for core in range(2):
+        lanes = slice(core * PACK, core * PACK + PACK)
+        found.append((first_parts[at * 2 + core].at[:, 0:SLOT, :], w_gate.at[:, :, lanes]))
+        for side in range(2):
+            found.append(
+                (
+                    second_parts[side * 2 + core].at[at * 4 : at * 4 + 4, 0:SLOT, :],
+                    w_up.at[side * 4 : side * 4 + 4, :, lanes],
+                )
+            )
+    return [
+        pltpu.make_async_copy(source, target, sems.at[n])
+        for n, (source, target) in enumerate(found)
+    ]
+
+
+def mlp_activations_kernel(
     here,
     normed,
     cotangent,
-    cotangent_turned,
     g0,
     g1,
     g2,
     g3,
-    d0,
-    d1,
-    d2,
-    d3,
-    out,
-    d_normed,
-    grads_zero,
-    grads_one,
-    down_zero,
-    down_one,
-    w_pair,
+    u0,
+    u1,
+    u2,
+    u3,
+    hidden_out,
+    d_gate_out,
+    d_up_out,
+    down_out,
+    w_gate,
+    w_up,
     down_raw,
-    w_down,
-    normed_turned,
-    hidden_all,
-    d_gate_all,
-    d_up_all,
-    grad_pair,
-    grad_down,
-    down_made,
     sem_pair,
     sem_down,
-    sem_grad,
-    sem_grad_down,
 ):
     step = pl.program_id(0)
     eighth_here, quarter_here = (here[0], here[1])
     side_here = eighth_here & 1
     slot = step & 1
-
-    def pair_copies(at, to, core):
+    first_parts, second_parts = ((g0, g1, g2, g3), (u0, u1, u2, u3))
+
+    def down_copies(at, to):
+        found = []
+        for core in range(2):
+            plane = ((2 * at + core) ^ quarter_here) ^ (eighth_here >> 1)
+            for side in range(2):
+                for quarter in range(REPS):
+                    target = down_raw.at[to, core, side, quarter]
+                    y, inner = (quarter >> 1, quarter & 1)
+                    found.append(
+                        (
+                            first_parts[quarter].at[side * 4 + plane, SLOT : SLOT + ROWS_A],
+                            target.at[0:ROWS_A],
+                        )
+                    )
+                    found.append(
+                        (
+                            second_parts[side * 2 + inner].at[y * 4 + plane, SLOT : SLOT + ROWS_A],
+                            target.at[ROWS_A : 2 * ROWS_A],
+                        )
+                    )
         return [
-            pltpu.make_async_copy(
-                (g0, g1, g2, g3)[side * 2 + core].at[pl.ds((at >> 1) * 4, 4)],
-                w_pair.at[to, side * 4 : side * 4 + 4],
-                sem_pair.at[to, side],
-            )
-            for side in range(2)
+            pltpu.make_async_copy(source, target, sem_down.at[to, n])
+            for n, (source, target) in enumerate(found)
         ]
 
-    def down_place(at, side):
-        return side * 4 + ((at ^ quarter_here) ^ (eighth_here >> 1))
-
-    def down_copies(at, to):
-        return [
-            pltpu.make_async_copy(
-                (d0, d1, d2, d3)[quarter].at[down_place(at, side)],
-                down_raw.at[to, side, quarter],
-                sem_down.at[to, side, quarter],
-            )
-            for side in range(2)
-            for quarter in range(REPS)
-        ]
-
-    def fetch(at, to):
-        for core in range(2):
-
-            @pl.when((at & 1) == core)
-            def _():
-                for copy in pair_copies(at, to, core):
-                    copy.start()
-
-        for copy in down_copies(at, to):
-            copy.start()
-
-    def grad_copies(at, to, core):
-        return [
-            pltpu.make_async_copy(
-                grad_pair.at[to, side * 4 : side * 4 + 4],
-                (grads_zero, grads_one)[core].at[side, pl.ds((at >> 1) * 4, 4)],
-                sem_grad.at[to, side],
-            )
-            for side in range(2)
-        ]
-
-    def grad_down_copies(at, to):
-        return [
-            pltpu.make_async_copy(
-                down_made.at[to, side, quarter],
-                (down_zero, down_one)[quarter & 1].at[quarter >> 1, down_place(at, side)],
-                sem_grad_down.at[to, side, quarter],
-            )
-            for side in range(2)
-            for quarter in range(REPS)
-        ]
-
-    def settle(at, to):
-        for copy in grad_copies(at, to, 0) + grad_down_copies(at, to):
-            copy.wait()
+    def pair_copies(at, to):
+        return pair_fetches(
+            first_parts, second_parts, at, w_gate.at[to], w_up.at[to], sem_pair.at[to]
+        )
 
     @pl.when(step == 0)
     def _():
-        fetch(step, slot)
-        normed_turned[...] = normed[...].T
-        out[...] = jnp.zeros_like(out)
-        d_normed[...] = jnp.zeros_like(d_normed)
-
-    for copy in pair_copies(step, slot, 0) + down_copies(step, slot):
-        copy.wait()
-
-    @pl.when(step + 1 < REPS)
-    def _():
-        fetch(step + 1, 1 - slot)
+        for at in range(2):
+            for copy in pair_copies(at, at) + down_copies(at, at):
+                copy.start()
+
+    for at in range(2):
+
+        @pl.when(step == at)
+        def _():
+            for copy in pair_copies(at, at) + down_copies(at, at):
+                copy.wait()
 
     def rows_of(quarter, which):
         eighth = (quarter ^ quarter_here) * 2 + which
         return pl.multiple_of(slot_of(eighth ^ eighth_here) * SLOT, SLOT)
 
-    for quarter in range(REPS):
-        lefts, rights = left_right(
-            down_raw[slot, side_here, quarter], down_raw[slot, 1 - side_here, quarter]
-        )
-        w_down[pl.ds(rows_of(quarter, 0), SLOT), :] = lefts
-        w_down[pl.ds(rows_of(quarter, 1), SLOT), :] = rights
-
-    tokens = normed.shape[0]
-    w_gate = w_pair[slot, :, 0:SLOT, :].reshape(WIDE, PACK)
-    w_up = w_pair[slot, :, SLOT : 2 * SLOT, :].reshape(WIDE, PACK)
+    for core in range(2):
+        lanes = slice(core * PACK, core * PACK + PACK)
+        for quarter in range(REPS):
+            lefts, rights = left_right(
+                down_raw[slot, core, side_here, quarter],
+                down_raw[slot, core, 1 - side_here, quarter],
+            )
+            down_out[0, pl.ds(rows_of(quarter, 0), SLOT), lanes] = lefts
+            down_out[0, pl.ds(rows_of(quarter, 1), SLOT), lanes] = rights
+
+    gate_weights = w_gate[slot].reshape(WIDE, 2 * PACK)
+    up_weights = w_up[slot].reshape(WIDE, 2 * PACK)
 
     def one_tile(t, carry):
         rows = pl.ds(pl.multiple_of(t * 256, 256), 256)
-        gate = dot_nn(normed[rows, :], w_gate)
-        up = dot_nn(normed[rows, :], w_up)
-        d_hidden = dot_nn(cotangent[rows, :], w_down[...])
+        gate = dot_nn(normed[rows, :], gate_weights)
+        up = dot_nn(normed[rows, :], up_weights)
+        d_hidden = dot_nn(cotangent[rows, :], down_out[0])
         sigmoid = 1.0 / (1.0 + jnp.exp(-gate))
         silu = gate * sigmoid
-        hidden = (silu * up).astype(bf16)
-        d_gate = (d_hidden * up * sigmoid * (1.0 + gate * (1.0 - sigmoid))).astype(bf16)
-        d_up = (d_hidden * silu).astype(bf16)
-        hidden_all[rows, :] = hidden
-        d_gate_all[rows, :] = d_gate
-        d_up_all[rows, :] = d_up
-        out[rows, :] += dot_nt(hidden, w_down[...])
-        d_normed[rows, :] += dot_nt(d_gate, w_gate) + dot_nt(d_up, w_up)
+        hidden_out[0, rows, :] = (silu * up).astype(bf16)
+        d_gate_out[0, rows, :] = (
+            d_hidden * up * sigmoid * (1.0 + gate * (1.0 - sigmoid))
+        ).astype(bf16)
+        d_up_out[0, rows, :] = (d_hidden * silu).astype(bf16)
         return carry
 
-    lax.fori_loop(0, tokens // 256, one_tile, 0)
-
-    @pl.when(step >= 2)
-    def _():
-        settle(step - 2, slot)
-
-    def grad_tile(t, carry):
-        rows = pl.ds(pl.multiple_of(t * 256, 256), 256)
-        two = pl.ds(t * 2, 2)
-        gate_part = dot_nn(normed_turned[rows, :], d_gate_all[...]).astype(bf16)
-        grad_pair[slot, two, 0:SLOT, :] = gate_part.reshape(2, SLOT, PACK)
-        up_part = dot_nn(normed_turned[rows, :], d_up_all[...]).astype(bf16)
-        grad_pair[slot, two, SLOT : 2 * SLOT, :] = up_part.reshape(2, SLOT, PACK)
-        grad_down[rows, :] = dot_nn(cotangent_turned[rows, :], hidden_all[...])
-        return carry
-
-    lax.fori_loop(0, WIDE // 256, grad_tile, 0)
-    for quarter in range(REPS):
-        lefts, rights = left_right(
-            grad_down[pl.ds(rows_of(quarter, 0), SLOT), :],
-            grad_down[pl.ds(rows_of(quarter, 1), SLOT), :],
-        )
-        down_made[slot, side_here, quarter] = lefts
-        down_made[slot, 1 - side_here, quarter] = rights
-    for core in range(2):
-
-        @pl.when((step & 1) == core)
-        def _():
-            for copy in grad_copies(step, slot, core):
-                copy.start()
-
-    for copy in grad_down_copies(step, slot):
-        copy.start()
-
-    @pl.when(step == REPS - 1)
-    def _():
-        settle(step - 1, 1 - slot)
-        settle(step, slot)
-
-
-def mlp(here, normed, cotangent, cotangent_turned, pair_parts, down_parts):
+    lax.fori_loop(0, normed.shape[0] // 256, one_tile, 0)
+
+
+def chunk_block(rows, columns):
+    return pl.BlockSpec((1, rows, columns), lambda i: (i, 0, 0))
+
+
+def mlp_activations(here, normed, cotangent, first_parts, second_parts):
     tokens = normed.shape[0]
-    pair_grads = jax.ShapeDtypeStruct((2, SLOTS, 2 * SLOT, PACK), bf16)
-    down_grads = jax.ShapeDtypeStruct((2, SLOTS, SLOT, PACK), bf16)
+    rows = jax.ShapeDtypeStruct((2, tokens, 2 * PACK), bf16)
     return pl.pallas_call(
-        mlp_kernel,
-        grid=(REPS,),
+        mlp_activations_kernel,
+        grid=(2,),
         in_specs=[
             pl.BlockSpec(memory_space=pltpu.SMEM),
             whole_block((tokens, WIDE)),
             whole_block((tokens, WIDE)),
-            whole_block((WIDE, tokens)),
         ]
         + [anywhere()] * 8,
-        out_specs=[whole_block((tokens, WIDE)), whole_block((tokens, WIDE))] + [anywhere()] * 4,
-        out_shape=[
-            jax.ShapeDtypeStruct((tokens, WIDE), f32),
-            jax.ShapeDtypeStruct((tokens, WIDE), f32),
-            pair_grads,
-            pair_grads,
-            down_grads,
-            down_grads,
-        ],
+        out_specs=[chunk_block(tokens, 2 * PACK)] * 3 + [chunk_block(WIDE, 2 * PACK)],
+        out_shape=[rows, rows, rows, jax.ShapeDtypeStruct((2, WIDE, 2 * PACK), bf16)],
         scratch_shapes=[
-            pltpu.VMEM((2, SLOTS, 2 * SLOT, PACK), bf16),
-            pltpu.VMEM((2, 2, REPS, SLOT, PACK), bf16),
-            pltpu.VMEM((WIDE, PACK), bf16),
-            pltpu.VMEM((WIDE, tokens), bf16),
-            pltpu.VMEM((tokens, PACK), bf16),
-            pltpu.VMEM((tokens, PACK), bf16),
-            pltpu.VMEM((tokens, PACK), bf16),
-            pltpu.VMEM((2, SLOTS, 2 * SLOT, PACK), bf16),
-            pltpu.VMEM((WIDE, PACK), f32),
-            pltpu.VMEM((2, 2, REPS, SLOT, PACK), bf16),
-            pltpu.SemaphoreType.DMA((2, 2)),
-            pltpu.SemaphoreType.DMA((2, 2, REPS)),
-            pltpu.SemaphoreType.DMA((2, 2)),
-            pltpu.SemaphoreType.DMA((2, 2, REPS)),
+            pltpu.VMEM((2, SLOTS, SLOT, 2 * PACK), bf16),
+            pltpu.VMEM((2, SLOTS, SLOT, 2 * PACK), bf16),
+            pltpu.VMEM((2, 2, 2, REPS, SLOT, PACK), bf16),
+            pltpu.SemaphoreType.DMA((2, 6)),
+            pltpu.SemaphoreType.DMA((2, 32)),
         ],
         compiler_params=pltpu.CompilerParams(vmem_limit_bytes=VMEM_BYTES),
         cost_estimate=pl.CostEstimate(
-            flops=44_000_000_000, bytes_accessed=44_000_000, transcendentals=2_000_000
+            flops=15_000_000_000, bytes_accessed=35_000_000, transcendentals=2_000_000
         ),
-        name="mlp",
-    )(here, normed, cotangent, cotangent_turned, *pair_parts, *down_parts)
+        name="mlp_activations",
+    )(here, normed, cotangent, *first_parts, *second_parts)
+
+
+def mlp_grads_kernel(
+    here,
+    normed,
+    cotangent_turned,
+    hidden,
+    d_gate,
+    d_up,
+    first_zero,
+    first_one,
+    second_zero,
+    second_one,
+    normed_turned,
+    grad_gate,
+    grad_up,
+    grad_down,
+    down_made,
+    sem_pair,
+    sem_down,
+):
+    step = pl.program_id(0)
+    eighth_here, quarter_here = (here[0], here[1])
+    side_here = eighth_here & 1
+    slot = step & 1
+    firsts, seconds = ((first_zero, first_one), (second_zero, second_one))
+
+    def copies(at, to):
+        found = []
+        for core in range(2):
+            found.append((grad_gate.at[to, core], firsts[core].at[at, :, 0:SLOT, :], sem_pair))
+            for side in range(2):
+                found.append(
+                    (
+                        grad_up.at[to, core, side * 4 : side * 4 + 4],
+                        seconds[core].at[side, at * 4 : at * 4 + 4, 0:SLOT, :],
+                        sem_pair,
+                    )
+                )
+        for core in range(2):
+            plane = ((2 * at + core) ^ quarter_here) ^ (eighth_here >> 1)
+            for side in range(2):
+                for quarter in range(REPS):
+                    source = down_made.at[to, core, side, quarter]
+                    y, inner = (quarter >> 1, quarter & 1)
+                    found.append(
+                        (
+                            source.at[0:ROWS_A],
+                            firsts[inner].at[y, side * 4 + plane, SLOT : SLOT + ROWS_A],
+                            sem_down,
+                        )
+                    )
+                    found.append(
+                        (
+                            source.at[ROWS_A : 2 * ROWS_A],
+                            seconds[inner].at[side, y * 4 + plane, SLOT : SLOT + ROWS_A],
+                            sem_down,
+                        )
+                    )
+        return [
+            pltpu.make_async_copy(source, target, sems.at[to, n])
+            for n, (source, target, sems) in enumerate(found)
+        ]
+
+    @pl.when(step == 0)
+    def _():
+        normed_turned[...] = normed[...].T
+
+    def grad_tile(t, carry):
+        rows = pl.ds(pl.multiple_of(t * 256, 256), 256)
+        two = pl.ds(t * 2, 2)
+        gate_part = dot_nn(normed_turned[rows, :], d_gate[0]).astype(bf16)
+        up_part = dot_nn(normed_turned[rows, :], d_up[0]).astype(bf16)
+        for core in range(2):
+            lanes = slice(core * PACK, core * PACK + PACK)
+            grad_gate[slot, core, two] = gate_part[:, lanes].reshape(2, SLOT, PACK)
+            grad_up[slot, core, two] = up_part[:, lanes].reshape(2, SLOT, PACK)
+        grad_down[rows, :] = dot_nn(cotangent_turned[rows, :], hidden[0])
+        return carry
+
+    lax.fori_loop(0, WIDE // 256, grad_tile, 0)
+
+    def rows_of(quarter, which):
+        eighth = (quarter ^ quarter_here) * 2 + which
+        return pl.multiple_of(slot_of(eighth ^ eighth_here) * SLOT, SLOT)
+
+    for core in range(2):
+        lanes = slice(core * PACK, core * PACK + PACK)
+        for quarter in range(REPS):
+            lefts, rights = left_right(
+                grad_down[pl.ds(rows_of(quarter, 0), SLOT), lanes],
+                grad_down[pl.ds(rows_of(quarter, 1), SLOT), lanes],
+            )
+            down_made[slot, core, side_here, quarter] = lefts
+            down_made[slot, core, 1 - side_here, quarter] = rights
+    for at in range(2):
+
+        @pl.when(step == at)
+        def _():
+            for copy in copies(at, at):
+                copy.start()
+
+    @pl.when(step == 1)
+    def _():
+        for at in range(2):
+            for copy in copies(at, at):
+                copy.wait()
+
+
+def mlp_grads(here, normed, cotangent_turned, hidden, d_gate, d_up):
+    tokens = normed.shape[0]
+    part = jax.ShapeDtypeStruct((2, SLOTS, SLOT + ROWS_A, PACK), bf16)
+    return pl.pallas_call(
+        mlp_grads_kernel,
+        grid=(2,),
+        in_specs=[
+            pl.BlockSpec(memory_space=pltpu.SMEM),
+            whole_block((tokens, WIDE)),
+            whole_block((WIDE, tokens)),
+        ]
+        + [chunk_block(tokens, 2 * PACK)] * 3,
+        out_specs=[anywhere()] * 4,
+        out_shape=[part] * 4,
+        scratch_shapes=[
+            pltpu.VMEM((WIDE, tokens), bf16),
+            pltpu.VMEM((2, 2, SLOTS, SLOT, PACK), bf16),
+            pltpu.VMEM((2, 2, SLOTS, SLOT, PACK), bf16),
+            pltpu.VMEM((WIDE, 2 * PACK), f32),
+            pltpu.VMEM((2, 2, 2, REPS, SLOT, PACK), bf16),
+            pltpu.SemaphoreType.DMA((2, 38)),
+            pltpu.SemaphoreType.DMA((2, 38)),
+        ],
+        compiler_params=pltpu.CompilerParams(vmem_limit_bytes=VMEM_BYTES),
+        cost_estimate=pl.CostEstimate(
+            flops=15_000_000_000, bytes_accessed=35_000_000, transcendentals=0
+        ),
+        name="mlp_grads",
+    )(here, normed, cotangent_turned, hidden, d_gate, d_up)
+
+
+def mlp_outputs_kernel(
+    hidden,
+    d_gate,
+    d_up,
+    w_down,
+    g0,
+    g1,
+    g2,
+    g3,
+    u0,
+    u1,
+    u2,
+    u3,
+    out,
+    d_normed,
+    w_gate,
+    w_up,
+    sem_pair,
+):
+    step = pl.program_id(0)
+    slot = step & 1
+
+    def pair_copies(at):
+        return pair_fetches(
+            (g0, g1, g2, g3), (u0, u1, u2, u3), at, w_gate.at[at], w_up.at[at], sem_pair.at[at]
+        )
+
+    @pl.when(step == 0)
+    def _():
+        for at in range(2):
+            for copy in pair_copies(at):
+                copy.start()
+
+    for at in range(2):
+
+        @pl.when(step == at)
+        def _():
+            for copy in pair_copies(at):
+                copy.wait()
+
+    gate_weights = w_gate[slot].reshape(WIDE, 2 * PACK)
+    up_weights = w_up[slot].reshape(WIDE, 2 * PACK)
+
+    def products(rows):
+        return (
+            dot_nt(hidden[0, rows, :], w_down[0]),
+            dot_nt(d_gate[0, rows, :], gate_weights) + dot_nt(d_up[0, rows, :], up_weights),
+        )
+
+    def tile_rows(t):
+        return pl.ds(pl.multiple_of(t * 256, 256), 256)
+
+    def first_tile(t, carry):
+        rows = tile_rows(t)
+        out[rows, :], d_normed[rows, :] = products(rows)
+        return carry
+
+    def second_tile(t, carry):
+        rows = tile_rows(t)
+        more_out, more_normed = products(rows)
+        out[rows, :] += more_out
+        d_normed[rows, :] += more_normed
+        return carry
+
+    tiles = out.shape[0] // 256
+
+    @pl.when(step == 0)
+    def _():
+        lax.fori_loop(0, tiles, first_tile, 0)
+
+    @pl.when(step == 1)
+    def _():
+        lax.fori_loop(0, tiles, second_tile, 0)
+
+
+def mlp_outputs(hidden, d_gate, d_up, w_down, first_parts, second_parts):
+    tokens = hidden.shape[1]
+    return pl.pallas_call(
+        mlp_outputs_kernel,
+        grid=(2,),
+        in_specs=[chunk_block(tokens, 2 * PACK)] * 3
+        + [chunk_block(WIDE, 2 * PACK)]
+        + [anywhere()] * 8,
+        out_specs=[whole_block((tokens, WIDE)), whole_block((tokens, WIDE))],
+        out_shape=[jax.ShapeDtypeStruct((tokens, WIDE), f32)] * 2,
+        scratch_shapes=[
+            pltpu.VMEM((2, SLOTS, SLOT, 2 * PACK), bf16),
+            pltpu.VMEM((2, SLOTS, SLOT, 2 * PACK), bf16),
+            pltpu.SemaphoreType.DMA((2, 6)),
+        ],
+        compiler_params=pltpu.CompilerParams(vmem_limit_bytes=VMEM_BYTES),
+        cost_estimate=pl.CostEstimate(
+            flops=15_000_000_000, bytes_accessed=35_000_000, transcendentals=0
+        ),
+        name="mlp_outputs",
+    )(hidden, d_gate, d_up, w_down, *first_parts, *second_parts)
 
 
 def attn_backward_kernel(
@@ -618,8 +774,6 @@
     probs_in,
     cosines,
     sines,
-    normed,
-    mixed,
     gains,
     spread,
     query_from,
@@ -629,24 +783,18 @@
     w_key_value,
     w_output,
     token_grad,
-    one_zero,
-    one_one,
-    two_zero,
-    two_one,
+    wire_in,
+    wire_out,
+    gain_sums,
     d_mixed_heads,
     head_parts,
     key_parts,
     value_parts,
     d_heads,
-    wire_in,
-    wire_out,
-    gain_sums,
 ):
     step = pl.program_id(0)
-    batches = pl.num_programs(0) - 1
-
-    @pl.when(step < batches)
-    def _():
+
+    def one_batch():
         gain_one = gains[0:1, :]
         gain_two = gains[1:2, :]
         mid = middle[...]
@@ -718,7 +866,6 @@
                 d_heads[:, place + c * 128 : place + c * 128 + 128] = joined.astype(bf16)
         d_query_low = d_heads[:, 0:1024]
         d_key_value_low = d_heads[:, 1024:1792]
-        rows = pl.ds(pl.multiple_of(step * MB_TOK, MB_TOK), MB_TOK)
         query_wire = dot_nt(d_query_low, query_from[...])
         key_value_wire = dot_nt(d_key_value_low, key_value_from[...])
         output_wire = dot_nt(d_branch, output_from[...]).astype(bf16)
@@ -726,12 +873,12 @@
             base = quarter * 512
             from_query = query_wire[:, quarter * 256 : quarter * 256 + 256]
             from_key = key_value_wire[:, quarter * 384 : quarter * 384 + 384]
-            wire_in[rows, base : base + 128] = from_query[:, 0:128].astype(bf16)
-            wire_in[rows, base + 128 : base + 256] = (
+            wire_in[:, base : base + 128] = from_query[:, 0:128].astype(bf16)
+            wire_in[:, base + 128 : base + 256] = (
                 from_query[:, 128:256] + from_key[:, 0:128]
             ).astype(bf16)
-            wire_in[rows, base + 256 : base + 512] = from_key[:, 128:384].astype(bf16)
-        wire_out[rows, :] = output_wire
+            wire_in[:, base + 256 : base + 512] = from_key[:, 128:384].astype(bf16)
+        wire_out[...] = output_wire
         d_normed = dot_nt(d_query_low, w_query[...]) + dot_nt(d_key_value_low, w_key_value[...])
         values = inputs[...].astype(f32)
         scale = lax.rsqrt(
@@ -750,34 +897,38 @@
         gain_sums[0:1, :] += term_one
         gain_sums[1:2, :] += term_two
 
-    @pl.when(step == batches)
-    def _():
-        normed_turned = normed[...].T
-        mixed_turned = mixed[...].T
-        row = lax.broadcasted_iota(jnp.int32, (SLOTS, 16, SLOT), 1)
-        gain_rows = jnp.zeros((SLOTS, 16, SLOT), f32)
-        for which in range(2):
-            spots = [
-                gain_sums[which : which + 1, s * SLOT : s * SLOT + SLOT].reshape(1, 1, SLOT)
-                for s in range(SLOTS)
-            ]
-            gain_rows = jnp.where(row == 8 + which, jnp.concatenate(spots, axis=0), gain_rows)
-        for quarter in range(REPS):
-            first = dot_nn(normed_turned, wire_in[:, quarter * 512 : quarter * 512 + 512])
-            second = dot_nn(mixed_turned, wire_out[:, quarter * 256 : quarter * 256 + 256])
-            block = jnp.concatenate(
-                [first[:, 0:384], first[:, 384:512] + second[:, 0:128], second[:, 128:256]], axis=1
-            ).reshape(SLOTS, SLOT, PACK)
-            y, core = (quarter >> 1, quarter & 1)
-            low_rows = block[:, 0:ROWS_A, :].astype(bf16)
-            high_rows = block[:, ROWS_A:SLOT, :].astype(bf16)
-            (one_zero, one_one)[core][y, :, :, :] = low_rows
-            target = (two_zero, two_one)[core]
-            tail = (block[:, 112:SLOT, 0:SLOT] + gain_rows).astype(bf16)
-            for side in range(2):
-                slots = slice(side * 4, side * 4 + 4)
-                target[side, y * 4 : y * 4 + 4, :, :] = high_rows[slots]
-                target[side, y * 4 : y * 4 + 4, 48:64, 0:SLOT] = tail[slots]
+    one_batch()
+
+
+def attn_grads_kernel(
+    normed, mixed, wire_in, wire_out, gain_sums, one_zero, one_one, two_zero, two_one
+):
+    normed_turned = normed[...].T
+    mixed_turned = mixed[...].T
+    row = lax.broadcasted_iota(jnp.int32, (SLOTS, 16, SLOT), 1)
+    gain_rows = jnp.zeros((SLOTS, 16, SLOT), f32)
+    for which in range(2):
+        spots = [
+            gain_sums[which : which + 1, s * SLOT : s * SLOT + SLOT].reshape(1, 1, SLOT)
+            for s in range(SLOTS)
+        ]
+        gain_rows = jnp.where(row == 8 + which, jnp.concatenate(spots, axis=0), gain_rows)
+    for quarter in range(REPS):
+        first = dot_nn(normed_turned, wire_in[:, quarter * 512 : quarter * 512 + 512])
+        second = dot_nn(mixed_turned, wire_out[:, quarter * 256 : quarter * 256 + 256])
+        block = jnp.concatenate(
+            [first[:, 0:384], first[:, 384:512] + second[:, 0:128], second[:, 128:256]], axis=1
+        ).reshape(SLOTS, SLOT, PACK)
+        y, core = (quarter >> 1, quarter & 1)
+        low_rows = block[:, 0:ROWS_A, :].astype(bf16)
+        high_rows = block[:, ROWS_A:SLOT, :].astype(bf16)
+        (one_zero, one_one)[core][y, :, :, :] = low_rows
+        target = (two_zero, two_one)[core]
+        tail = (block[:, 112:SLOT, 0:SLOT] + gain_rows).astype(bf16)
+        for side in range(2):
+            slots = slice(side * 4, side * 4 + 4)
+            target[side, y * 4 : y * 4 + 4, :, :] = high_rows[slots]
+            target[side, y * 4 : y * 4 + 4, 48:64, 0:SLOT] = tail[slots]
 
 
 def attn_backward(
@@ -790,8 +941,6 @@
     value_both,
     probs,
     tables,
-    normed,
-    mixed,
     gains,
     places,
     weights,
@@ -800,12 +949,11 @@
     count = tokens // MB_TOK
 
     def per_batch(columns):
-        return pl.BlockSpec((MB_TOK, columns), lambda i: (jnp.minimum(i, count - 1), 0))
-
-    half = jax.ShapeDtypeStruct((2, SLOTS, ROWS_A, PACK), bf16)
+        return pl.BlockSpec((MB_TOK, columns), lambda i: (i, 0))
+
     return pl.pallas_call(
         attn_backward_kernel,
-        grid=(count + 1,),
+        grid=(count,),
         in_specs=[
             per_batch(WIDE),
             per_batch(WIDE),
@@ -814,32 +962,35 @@
             per_batch(WIDE),
             per_batch(PACK),
             per_batch(PACK),
-            pl.BlockSpec(
-                (1, KV_HEADS, MB_TOK, 768), lambda i: (jnp.minimum(i, count - 1), 0, 0, 0)
-            ),
+            pl.BlockSpec((1, KV_HEADS, MB_TOK, 768), lambda i: (i, 0, 0, 0)),
             per_batch(128),
             per_batch(128),
-            whole_block((tokens, WIDE)),
-            whole_block((tokens, WIDE)),
             whole_block((8, WIDE)),
         ]
         + [whole_block(place.shape) for place in places]
         + [whole_block(weight.shape) for weight in weights],
-        out_specs=[per_batch(D)] + [whole_block(half.shape)] * 4,
-        out_shape=[jax.ShapeDtypeStruct((tokens, D), bf16), half, half, half, half],
+        out_specs=[
+            per_batch(D),
+            per_batch(REPS * 512),
+            per_batch(REPS * 256),
+            whole_block((8, WIDE)),
+        ],
+        out_shape=[
+            jax.ShapeDtypeStruct((tokens, D), bf16),
+            jax.ShapeDtypeStruct((tokens, REPS * 512), bf16),
+            jax.ShapeDtypeStruct((tokens, REPS * 256), bf16),
+            jax.ShapeDtypeStruct((8, WIDE), f32),
+        ],
         scratch_shapes=[
             pltpu.VMEM((MB_TOK, WIDE), bf16),
             pltpu.VMEM((HEADS, MB_TOK, 128), f32),
             pltpu.VMEM((KV_HEADS, MB_TOK, 128), f32),
             pltpu.VMEM((KV_HEADS, MB_TOK, 128), f32),
             pltpu.VMEM((MB_TOK, 1792), bf16),
-            pltpu.VMEM((tokens, REPS * 512), bf16),
-            pltpu.VMEM((tokens, REPS * 256), bf16),
-            pltpu.VMEM((8, WIDE), f32),
         ],
         compiler_params=pltpu.CompilerParams(vmem_limit_bytes=VMEM_BYTES),
         cost_estimate=pl.CostEstimate(
-            flops=40_000_000_000, bytes_accessed=50_000_000, transcendentals=0
+            flops=32_000_000_000, bytes_accessed=40_000_000, transcendentals=0
         ),
         name="attn_backward",
     )(
@@ -852,33 +1003,61 @@
         value_both,
         probs,
         *tables,
-        normed,
-        mixed,
         gains,
         *places,
         *weights,
     )
 
 
-Z_NEAR = ("fsdp", 1)
-Z_FAR = ("fsdp", 2)
-X_SIDE = ("fsdp", 0)
-Y_SIDE = ("rep", 1)
-CORE = ("rep", 0)
+def attn_grads(normed, mixed, wire_in, wire_out, gain_sums):
+    half = jax.ShapeDtypeStruct((2, SLOTS, ROWS_A, PACK), bf16)
+    arrays = (normed, mixed, wire_in, wire_out, gain_sums)
+    return pl.pallas_call(
+        attn_grads_kernel,
+        grid=(1,),
+        in_specs=[whole_block(array.shape) for array in arrays],
+        out_specs=[whole_block(half.shape)] * 4,
+        out_shape=[half] * 4,
+        compiler_params=pltpu.CompilerParams(vmem_limit_bytes=VMEM_BYTES),
+        cost_estimate=pl.CostEstimate(
+            flops=8_000_000_000, bytes_accessed=14_000_000, transcendentals=0
+        ),
+        name="attn_grads",
+    )(*arrays)
+
+
+X_SIDE = ("fsdp", 1)
+Y_SIDE = ("rep", 2)
+CORE = ("rep", 1)
 
 
 def swap_with(values, step):
-    axis, bit = step
+    axis, mask = step
     count = lax.axis_size(axis)
-    return lax.ppermute(values, axis, [(i, i ^ (1 << bit)) for i in range(count)])
-
-
-def gather_parts(block, side_first):
-    two = jnp.stack([block, swap_with(block, Z_NEAR)])
-    four = jnp.concatenate([two, swap_with(two, Z_FAR)])
-    first, second = (X_SIDE, Y_SIDE) if side_first else (Y_SIDE, X_SIDE)
-    eight = jnp.concatenate([four, swap_with(four, first)])
-    across = swap_with(eight, second)
+    return lax.ppermute(values, axis, [(i, i ^ mask) for i in range(count)])
+
+
+def after(values, *done):
+    return lax.optimization_barrier((values, done))[0]
+
+
+def along_z(block):
+    return jnp.stack([block] + [swap_with(block, ("fsdp", 2 * k)) for k in range(1, 4)])
+
+
+def sides_of(side_first):
+    return (X_SIDE, Y_SIDE) if side_first else (Y_SIDE, X_SIDE)
+
+
+def along_first(four, side_first):
+    return jnp.concatenate([four, swap_with(four, sides_of(side_first)[0])])
+
+
+def along_second(eight, side_first):
+    return swap_with(eight, sides_of(side_first)[1])
+
+
+def along_core(eight, across):
     return (eight, swap_with(eight, CORE), across, swap_with(across, CORE))
 
 
@@ -886,17 +1065,29 @@
     return (left.astype(f32) + right.astype(f32)).astype(bf16)
 
 
-def scatter_parts(kept, sent, side_first):
-    first, second = (X_SIDE, Y_SIDE) if side_first else (Y_SIDE, X_SIDE)
-    came = swap_with(sent, CORE)
-    came_next = swap_with(added(kept[1], came[1]), second)
-    eight = added(kept[0], came[0])
-    came = swap_with(added(eight[4:8], came_next[4:8]), first)
-    four = added(eight[0:4], came_next[0:4])
-    came_next = swap_with(added(four[2:4], came[2:4]), Z_FAR)
-    two = added(four[0:2], came[0:2])
-    came = swap_with(added(two[1], came_next[1]), Z_NEAR)
-    return two[0].astype(f32) + came_next[0].astype(f32) + came.astype(f32)
+class Reduction:
+    def __init__(self, kept, sent, side_first):
+        self.kept = kept
+        self.sent = sent
+        self.first, self.second = sides_of(side_first)
+
+    def over_core(self):
+        came = swap_with(self.sent, CORE)
+        self.out = added(self.kept[1], came[1])
+        self.eight = added(self.kept[0], came[0])
+
+    def over_second(self):
+        came = swap_with(self.out, self.second)
+        self.out = added(self.eight[4:8], came[4:8])
+        self.four = added(self.eight[0:4], came[0:4])
+
+    def over_first(self):
+        came = swap_with(self.out, self.first)
+        self.blocks = [added(self.four[k], came[k]) for k in range(4)]
+
+    def over_z(self):
+        came = [swap_with(self.blocks[k], ("fsdp", 2 * k)) for k in range(1, 4)]
+        return sum((block.astype(f32) for block in came), self.blocks[0].astype(f32))
 
 
 def split_parts(blocks, side_first):
@@ -927,15 +1118,19 @@
     return jnp.concatenate([matrices, gains], axis=0)
 
 
-def pair_block(w_gate, w_up):
-    taller = ((0, SLOT - USED), (0, 0))
-    return jnp.concatenate([jnp.pad(w_gate, taller), jnp.pad(w_up, taller)], axis=0)
-
-
 def down_block(w_down):
     halves = w_down.T.reshape(2, USED, HALF_PACK)
     halves = jnp.concatenate([halves[0], halves[1]], axis=1)
     return jnp.pad(halves, ((0, SLOT - USED), (0, 0)))
+
+
+def mlp_blocks(w_gate, w_up, w_down):
+    taller = ((0, SLOT - USED), (0, 0))
+    down = down_block(w_down)
+    return (
+        jnp.concatenate([jnp.pad(w_gate, taller), down[:ROWS_A]], axis=0),
+        jnp.concatenate([jnp.pad(w_up, taller), down[ROWS_A:]], axis=0),
+    )
 
 
 def down_of(block):
@@ -986,10 +1181,20 @@
         eighth_here = lax.axis_index("fsdp").astype(jnp.int32)
         quarter_here = lax.axis_index("rep").astype(jnp.int32)
         attn_pack = attn_block(w_query, w_key, w_value, w_output, attn_gain, mlp_gain)
-        first_parts = gather_parts(attn_pack[:ROWS_A], True)
-        second_parts = gather_parts(attn_pack[ROWS_A:], False)
-        pair_parts = gather_parts(pair_block(w_gate, w_up), False)
-        down_parts = gather_parts(down_block(w_down), True)
+        mlp_first, mlp_second = mlp_blocks(w_gate, w_up, w_down)
+        one, two = (along_z(attn_pack[:ROWS_A]), along_z(attn_pack[ROWS_A:]))
+        mlp_first, mlp_second = after((mlp_first, mlp_second), one, two)
+        three, four = (along_z(mlp_first), along_z(mlp_second))
+        one, two = (along_first(one, True), along_first(two, False))
+        one_across, two_across = (along_second(one, True), along_second(two, False))
+        first_parts = along_core(one, one_across)
+        second_parts = along_core(two, two_across)
+        three, four = after((three, four), one_across, two_across)
+        three, four = (along_first(three, True), along_first(four, False))
+        first_parts, second_parts = after((first_parts, second_parts), three, four)
+        three_across, four_across = (along_second(three, True), along_second(four, False))
+        mlp_first_parts = along_core(three, three_across)
+        mlp_second_parts = along_core(four, four_across)
     else:
         eighth_here = jnp.int32(0)
         quarter_here = jnp.int32(0)
@@ -1003,10 +1208,15 @@
         )
         first_parts = split_parts(attn_blocks[:, :, :ROWS_A], True)
         second_parts = split_parts(attn_blocks[:, :, ROWS_A:], False)
-        pair_parts = split_parts(
-            every_block(lambda e, q: pair_block(cut(mats[4], e, q), cut(mats[5], e, q))), False
-        )
-        down_parts = split_parts(every_block(lambda e, q: down_block(cut(mats[6], e, q))), True)
+        mlp_each = [
+            [
+                mlp_blocks(cut(mats[4], e, q), cut(mats[5], e, q), cut(mats[6], e, q))
+                for q in range(REPS)
+            ]
+            for e in range(SLOTS)
+        ]
+        mlp_first_parts = split_parts(every_block(lambda e, q: mlp_each[e][q][0]), True)
+        mlp_second_parts = split_parts(every_block(lambda e, q: mlp_each[e][q][1]), False)
     here = jnp.stack([eighth_here, quarter_here])
     places = placing(eighth_here, quarter_here)
     spread = places[0]
@@ -1014,6 +1224,7 @@
     tables = rope_tables(positions.reshape(-1))
     inputs = jnp.dot(tokens, spread[:D], preferred_element_type=f32).astype(bf16)
     upstream = jnp.dot(cotangent, spread[:D], preferred_element_type=f32).astype(bf16)
+    upstream_turned = upstream.T
     (
         normed,
         query_rot,
@@ -1026,13 +1237,23 @@
         *weights,
         gains,
     ) = attn_forward(inputs, places, tables, segments, first_parts, second_parts)
-    mlp_out, d_normed_two, pair_kept, pair_sent, down_kept, down_sent = mlp(
-        here, normed_two, upstream, upstream.T, pair_parts, down_parts
-    )
-    output = jnp.dot(
-        (middle + mlp_out).astype(bf16), spread[:D].T, preferred_element_type=f32
-    ).astype(bf16)
-    token_grad, one_kept, one_sent, two_kept, two_sent = attn_backward(
+    hidden, d_gate, d_up, w_down_all = mlp_activations(
+        here, normed_two, upstream, mlp_first_parts, mlp_second_parts
+    )
+    three_kept, three_sent, four_kept, four_sent = mlp_grads(
+        here, normed_two, upstream_turned, hidden, d_gate, d_up
+    )
+    three = Reduction(three_kept, three_sent, True)
+    four = Reduction(four_kept, four_sent, False)
+    hidden, d_gate, d_up = after((hidden, d_gate, d_up), three_kept, four_kept)
+    mlp_out, d_normed_two = mlp_outputs(
+        hidden, d_gate, d_up, w_down_all, mlp_first_parts, mlp_second_parts
+    )
+    if paired:
+        three.over_core()
+        four.over_core()
+        d_normed_two = after(d_normed_two, three.out, four.out)
+    token_grad, wire_in, wire_out, gain_parts = attn_backward(
         upstream,
         middle,
         d_normed_two,
@@ -1042,17 +1263,35 @@
         value_both,
         probs,
         tables,
-        normed,
-        mixed,
         gains,
         places,
         weights,
     )
     if paired:
-        down_sum = scatter_parts(down_kept, down_sent, True)
-        pair_sum = scatter_parts(pair_kept, pair_sent, False)
-        first_sum = scatter_parts(one_kept, one_sent, True)
-        second_sum = scatter_parts(two_kept, two_sent, False)
+        three.over_second()
+        four.over_second()
+        wire_in = after(wire_in, three.out, four.out)
+    one_kept, one_sent, two_kept, two_sent = attn_grads(
+        normed, mixed, wire_in, wire_out, gain_parts
+    )
+    output = jnp.dot(
+        (middle + mlp_out).astype(bf16), spread[:D].T, preferred_element_type=f32
+    ).astype(bf16)
+    if paired:
+        one = Reduction(one_kept, one_sent, True)
+        two = Reduction(two_kept, two_sent, False)
+        one.over_core()
+        two.over_core()
+        three.over_first()
+        four.over_first()
+        one.over_second()
+        two.over_second()
+        three_sum = three.over_z()
+        four_sum = four.over_z()
+        one.over_first()
+        two.over_first()
+        first_sum = one.over_z()
+        second_sum = two.over_z()
         attn_sum = jnp.concatenate([first_sum, second_sum], axis=0)
         gain_sums = (attn_sum[USED, :USED], attn_sum[USED + 1, :USED])
         attn_sum = attn_sum[:USED]
@@ -1061,9 +1300,9 @@
             attn_sum[:, 240:320],
             attn_sum[:, 320:400],
             attn_sum[:, 400:640],
-            pair_sum[:USED],
-            pair_sum[SLOT : SLOT + USED],
-            down_of(down_sum),
+            three_sum[:USED],
+            four_sum[:USED],
+            down_of(jnp.concatenate([three_sum[SLOT:], four_sum[SLOT:]], axis=0)),
         ]
     else:
         attn_blocks = jnp.concatenate(
@@ -1082,15 +1321,16 @@
             for which in range(2)
         )
         attn_blocks = attn_blocks[:, :, :USED]
-        pair_blocks = join_parts(pair_kept, pair_sent, False)
-        down_blocks = join_parts(down_kept, down_sent, True)
+        three_blocks = join_parts(three_kept, three_sent, True)
+        four_blocks = join_parts(four_kept, four_sent, False)
+        down_blocks = jnp.concatenate([three_blocks[:, :, SLOT:], four_blocks[:, :, SLOT:]], axis=2)
         grads = [
             owned(attn_blocks[..., 0:240]),
             owned(attn_blocks[..., 240:320]),
             owned(attn_blocks[..., 320:400]),
             owned(attn_blocks[..., 400:640]),
-            owned(pair_blocks[:, :, :USED]),
-            owned(pair_blocks[:, :, SLOT : SLOT + USED]),
+            owned(three_blocks[:, :, :USED]),
+            owned(four_blocks[:, :, :USED]),
             owned(jax.vmap(jax.vmap(down_of))(down_blocks)),
         ]
     return (

time: 514 us -> 415 us (0.81)
  waiting for transfers between devices: 240 us -> 95 us
  starting transfers between devices: 43.1 us -> 69.2 us
  local copies, waits for them, and re-layouts: 14.3 us -> 28.2 us
  Pallas kernels: 149 us -> 161 us
  other arithmetic: 50.9 us -> 43.2 us
    ppermute x44 -> x52, waiting for transfers between devices: 240 us -> 95 us  [swap_with(): return lax.ppermute(values, axis, [(i, i ^ mask) for i in range(count)])]
    ppermute x44 -> x52, starting transfers between devices: 43.1 us -> 69.2 us  [swap_with(): return lax.ppermute(values, axis, [(i, i ^ mask) for i in range(count)])]
    concatenate x9 -> x1, other arithmetic: 11.6 us -> 0.04 us  [mlp_blocks(): jnp.concatenate([jnp.pad(w_gate, taller), down[:ROWS_A]], axis=0)]
    pallas_call x2 -> x5, Pallas kernels: 114 us -> 125 us  [the longest x1 41.5 us: attn_backward(): pl.pallas_call(attn_backward_kernel, grid=(count,), in_specs=[per_batch(W...]
    unnamed x44 -> x68, local copies, waits for them, and re-layouts: 9.59 us -> 17.9 us
    convert_element_type x16 -> x12, other arithmetic: 19.5 us -> 23 us  [added(): return (left.astype(f32) + right.astype(f32)).astype(bf16)]
  transfers between devices with their start and end apart: 44 -> 52, of which waited for: 19 -> 15; matrix products, arithmetic and copies ran while one was open for 14% -> 18% of each run, Pallas kernels for 16% -> 27%
where the time goes in v2:
time: 415 us; the launch traced here: 411 us
  Pallas kernels  161 us (39%)
  waiting for transfers between devices  95 us (23%)
  starting transfers between devices  69.2 us (17%)
  other arithmetic  43.2 us (10%)
  local copies, waits for them, and re-layouts  28.2 us (7%)
  matrix products  13.2 us (3%)
    ppermute x52, waiting for transfers between devices, swap_with(): return lax.ppermute(values, axis, [(i, i ^ mask) for i in range(count)])  95 us
    ppermute x52, starting transfers between devices, swap_with(): return lax.ppermute(values, axis, [(i, i ^ mask) for i in range(count)])  69.2 us
    pallas_call x1, Pallas kernels, attn_backward(): pl.pallas_call(attn_backward_kernel, grid=(count,), in_specs=[per_batch(W...  41.5 us
    pallas_call x1, Pallas kernels, attn_forward(): pl.pallas_call(attn_forward_kernel, grid=(count,), in_specs=[per_batch(WI...  35.1 us
    pallas_call x1, Pallas kernels, mlp_activations(): pl.pallas_call(mlp_activations_kernel, grid=(2,), in_specs=[pl.BlockSpec(...  25 us
    pallas_call x1, Pallas kernels, mlp_outputs(): pl.pallas_call(mlp_outputs_kernel, grid=(2,), in_specs=[chunk_block(token...  24.4 us
    pallas_call x1, Pallas kernels, mlp_grads(): pl.pallas_call(mlp_grads_kernel, grid=(2,), in_specs=[pl.BlockSpec(memory...  24.2 us
    convert_element_type x12, other arithmetic, added(): return (left.astype(f32) + right.astype(f32)).astype(bf16)  23 us
  transfers between devices with their start and end apart: 52, of which 15 were waited for; matrix products, arithmetic and copies ran while one was open for 18% of the time, Pallas kernels for 27%

profile of v2, /device:TPU:0, one launch (start us, length us, event | category | flops | bytes accessed | tf_op | source)
XLA Modules:
  0.0 410.8 jit_solution(12991261753230256732)
XLA Ops:
  10.4 3.8 collective-permute-start.9
  20.0 4.9 %collective-permute-done.8 = bf16[64,640]{1,0:T(8,128)(2,1)S(1)} collective-permute-done((bf16[64,640]{1,0:T(8,128)(2,1)S(1)}, bf16[64,640]{1,0:T(8,128)(2,1)S(1)}, u32[]{:S(2)}, u32[]{:S(2)}) %collective-permute-start.8) | collective-permute-done | bytes 81952 | tf_op jit(solution)/shard_map/ppermute | solution.py:1037
  48.9 4.7 %collective-permute-done.14 = bf16[192,640]{1,0:T(8,128)(2,1)S(1)} collective-permute-done((bf16[192,640]{1,0:T(8,128)(2,1)S(1)}, bf16[192,640]{1,0:T(8,128)(2,1)S(1)}, u32[]{:S(2)}, u32[]{:S(2)}) %collective-permute-start.14) | collective-permute-done | bytes 245792 | tf_op jit(solution)/shard_map/ppermute | solution.py:1037
  53.6 12.9 %collective-permute-done.15 = bf16[192,640]{1,0:T(8,128)(2,1)S(1)} collective-permute-done((bf16[192,640]{1,0:T(8,128)(2,1)S(1)}, bf16[192,640]{1,0:T(8,128)(2,1)S(1)}, u32[]{:S(2)}, u32[]{:S(2)}) %collective-permute-start.15) | collective-permute-done | bytes 245792 | tf_op jit(solution)/shard_map/ppermute | solution.py:1037
  74.2 4.3 %fusion.18 = bf16[1024,768]{0,1:T(8,128)(2,1)} fusion(bf16[768,960]{0,1:T(8,128)(2,1)S(1)} %copy-done, pred[1024,1024]{1,0:T(32,128)(4,1)} %get-tuple-element.199), kind=kOutput, calls=%fused_computation.29 | convolution fusion | flops 1510735872 | bytes 4030464 | tf_op jit(solution)/shard_map/dot_general | solution.py:1226
  80.6 7.3 %collective-permute-done.21 = bf16[4,192,640]{2,1,0:T(8,128)(2,1)} collective-permute-done((bf16[4,192,640]{2,1,0:T(8,128)(2,1)S(1)}, bf16[4,192,640]{2,1,0:T(8,128)(2,1)}, u32[]{:S(2)}, u32[]{:S(2)}) %collective-permute-start.21) | collective-permute-done | bytes 983072 | tf_op jit(solution)/shard_map/ppermute | solution.py:1037
  91.8 3.8 collective-permute-done.20
  114.4 19.7 %collective-permute-done.26.u2 = bf16[8,192,640]{2,1,0:T(8,128)(2,1)} collective-permute-done((bf16[8,192,640]{2,1,0:T(8,128)(2,1)}, bf16[8,192,640]{2,1,0:T(8,128)(2,1)}, u32[]{:S(2)}, u32[]{:S(2)}) %collective-permute-start.26) | collective-permute-done | bytes 1966112 | tf_op jit(solution)/shard_map/ppermute | solution.py:1037
  134.6 35.1 %attn_forward.1 = (bf16[768,1024]{1,0:T(8,128)(2,1)}, bf16[768,1024]{1,0:T(8,128)(2,1)}, bf16[768,640]{1,0:T(8,128)(2,1)}, bf16[768,640]{1,0:T(8,128)(2,1)}, bf1...) custom-call(bf16[768,1024]{1,0:T(8,128)(2,1)} %fusion.24.inputs, ...), custom_call_target="tpu_custom_call" | custom-call | flops 24000000000 | bytes 40000000 | tf_op jit(solution)/shard_map/attn_forward/pallas_call | solution.py:315
  171.7 25.0 %mlp_activations.1 = (bf16[2,768,1280]{2,1,0:T(8,128)(2,1)}, bf16[2,768,1280]{2,1,0:T(8,128)(2,1)}, bf16[2,768,1280]{2,1,0:T(8,128)(2,1)}, bf16[2,1024,1280]{2,1,0:T(8,128)(2,1)}) custom-call(s32[2]{0:T(128)} %pad_add_fusion.1.here, bf16[768,1024]{1,0:T(8,128)(2,1)} %get-tuple-element.71.normed, bf16[768,1024]{1,0:T(8,128)(2,1)} %bitcast.140, ...), custom_call_target="tpu_custom_call" | custom-call | flops 15000000512 | bytes 35000000 | tf_op jit(solution)/shard_map/mlp_activations/pallas_call | solution.py:504
  196.7 24.2 %mlp_grads.1 = (bf16[2,8,192,640]{3,2,1,0:T(8,128)(2,1)}, bf16[2,8,192,640]{3,2,1,0:T(8,128)(2,1)}, bf16[2,8,192,640]{3,2,1,0:T(8,128)(2,1)}, bf16[2,8,192,640]{3,2,1,0:T(8,128)(2,1)}) custom-call(s32[2]{0:T(128)} %pad_add_fusion.1.here, bf16[768,1024]{1,0:T(8,128)(2,1)} %get-tuple-element.71.normed, bf16[1024,768]{1,0:T(8,128)(2,1)} %copy.68.cotangent_turned, ...), custom_call_target="tpu_custom_call" | custom-call | flops 15000000512 | bytes 35000000 | tf_op jit(solution)/shard_map/mlp_grads/pallas_call | solution.py:640
  221.4 24.4 %mlp_outputs.1 = (f32[768,1024]{1,0:T(8,128)}, f32[768,1024]{1,0:T(8,128)}) custom-call(bf16[2,768,1280]{2,1,0:T(8,128)(2,1)} %get-tuple-element.77.hidden, bf16[2,768,1280]{2,1,0:T(8,128)(2,1)} %get-tuple-element.78.d_gate, bf16[2,768,1280]{2,1,0:T(8,128)(2,1)} %get-tuple-element.79.d_up, bf16[2,1024,1280]{2,1,0:T(8,128)(2,1)} %get-tuple-element.80.w_down, ...), custom_call_target="tpu_custom_call" | custom-call | flops 15000000512 | bytes 35000000 | tf_op jit(solution)/shard_map/mlp_outputs/pallas_call | solution.py:745
  245.9 5.9 %add_convert_fusion = (bf16[1,8,192,640]{3,2,1,0:T(8,128)(2,1)S(1)}, bf16[8,192,640]{2,1,0:T(8,128)(2,1)}) fusion(bf16[2,8,192,640]{3,2,1,0:T(8,128)(2,1)} %collective-permute-done.29, bf16[2,8,192,640]{3,2,1,0:T(8,128)(2,1)} %get-tuple-element.76), kind=kLoop, calls=%fused_computation.7 | loop fusion | flops 7864320 | bytes 11796480 | tf_op jit(solution)/shard_map/convert_element_type | solution.py:1065
  253.3 4.7 %add_convert_fusion.1 = (bf16[1,8,192,640]{3,2,1,0:T(8,128)(2,1)S(1)}, bf16[8,192,640]{2,1,0:T(8,128)(2,1)}) fusion(bf16[2,8,192,640]{3,2,1,0:T(8,128)(2,1)} %collective-permute-done.28, bf16[2,8,192,640]{3,2,1,0:T(8,128)(2,1)S(1)} %copy-done.2), kind=kLoop, calls=%fused_computation.8 | loop fusion | flops 7864320 | bytes 11796480 | tf_op jit(solution)/shard_map/convert_element_type | solution.py:1065
  258.4 41.5 %attn_backward.1 = (bf16[768,960]{1,0:T(8,128)(2,1)}, bf16[768,2048]{1,0:T(8,128)(2,1)}, bf16[768,1024]{1,0:T(8,128)(2,1)}, f32[8,1024]{1,0:T(8,128)}) custom-call(bf16[768,1024]{1,0:T(8,128)(2,1)} %bitcast.141, f32[768,1024]{1,0:T(8,128)} %get-tuple-element.70.middle, f32[768,1024]{1,0:T(8,128)} %get-tuple-element.85.d_normed_two, ...), custom_call_target="tpu_custom_call" | custom-call | flops 32000000000 | bytes 40000000 | tf_op jit(solution)/shard_map/attn_backward/pallas_call | solution.py:954
  307.7 10.4 %attn_grads.1 = (bf16[2,8,64,640]{3,2,1,0:T(8,128)(2,1)}, bf16[2,8,64,640]{3,2,1,0:T(8,128)(2,1)}, bf16[2,8,64,640]{3,2,1,0:T(8,128)(2,1)}, bf16[2,8,64,640]{3,2,1,0:T(8,128)(2,1)}) custom-call(bf16[768,1024]{1,0:T(8,128)(2,1)} %get-tuple-element.95.normed, bf16[768,1024]{1,0:T(8,128)(2,1)} %get-tuple-element.96.mixed, ...), custom_call_target="tpu_custom_call" | custom-call | flops 8000000000 | bytes 14000000 | tf_op jit(solution)/shard_map/attn_grads/pallas_call | solution.py:1015
  318.9 5.7 %fusion.21 = bf16[768,960]{0,1:T(8,128)(2,1)} fusion(pred[1024,1024]{1,0:T(32,128)(4,1)S(1)} %copy-done.11, f32[768,1024]{1,0:T(8,128)} %get-tuple-element.70.middle, f32[768,1024]{1,0:T(8,128)} %get-tuple-element.81), kind=kOutput, calls=%fused_computation.30 | convolution fusion | flops 1512259584 | bytes 8749056 | tf_op jit(solution)/shard_map/dot_general | solution.py:1277
  327.4 6.1 %collective-permute-start.49 = (bf16[192,640]{1,0:T(8,128)(2,1)S(1)}, bf16[192,640]{1,0:T(8,128)(2,1)S(1)}, u32[]{:S(2)}, u32[]{:S(2)}) collective-permute-start(bf16[192,640]{1,0:T(8,128)(2,1)S(1)} %get-tuple-element.167), channel_id=1, source_target_pairs={{0,8},{4,12},{8,0},{12,4},{16,24},{20,28},{24,16},{28,20},{1,9},{5... | collective-permute-start | bytes 737288 | tf_op jit(solution)/shard_map/ppermute | solution.py:1037
  334.3 8.3 %collective-permute-done.44 = bf16[4,192,640]{2,1,0:T(8,128)(2,1)} collective-permute-done((bf16[4,192,640]{2,1,0:T(8,128)(2,1)}, bf16[4,192,640]{2,1,0:T(8,128)(2,1)}, u32[]{:S(2)}, u32[]{:S(2)}) %collective-permute-start.44) | collective-permute-done | bytes 983072 | tf_op jit(solution)/shard_map/ppermute | solution.py:1037
  346.2 5.1 %collective-permute-start.45 = (bf16[192,640]{1,0:T(8,128)(2,1)S(1)}, bf16[192,640]{1,0:T(8,128)(2,1)S(1)}, u32[]{:S(2)}, u32[]{:S(2)}) collective-permute-start(bf16[192,640]{1,0:T(8,128)(2,1)S(1)} %get-tuple-element.170), channel_id=1, source_target_pairs={{0,8},{4,12},{8,0},{12,4},{16,24},{20,28},{24,16},{28,20},{1,9},{5... | collective-permute-start | bytes 737288 | tf_op jit(solution)/shard_map/ppermute | solution.py:1037
  360.2 14.0 %collective-permute-done.46 = bf16[192,640]{1,0:T(8,128)(2,1)S(1)} collective-permute-done((bf16[192,640]{1,0:T(8,128)(2,1)S(1)}, bf16[192,640]{1,0:T(8,128)(2,1)S(1)}, u32[]{:S(2)}, u32[]{:S(2)}) %collective-permute-start.46) | collective-permute-done | bytes 245792 | tf_op jit(solution)/shard_map/ppermute | solution.py:1037
  380.4 5.9 %collective-permute-done.40 = bf16[4,64,640]{2,1,0:T(8,128)(2,1)S(1)} collective-permute-done((bf16[4,64,640]{2,1,0:T(8,128)(2,1)}, bf16[4,64,640]{2,1,0:T(8,128)(2,1)S(1)}, u32[]{:S(2)}, u32[]{:S(2)}) %collective-permute-start.40) | collective-permute-done | bytes 327712 | tf_op jit(solution)/shard_map/ppermute | solution.py:1037
  386.4 6.1 %collective-permute-start.41 = (bf16[64,640]{1,0:T(8,128)(2,1)S(1)}, bf16[64,640]{1,0:T(8,128)(2,1)S(1)}, u32[]{:S(2)}, u32[]{:S(2)}) collective-permute-start(bf16[64,640]{1,0:T(8,128)(2,1)S(1)} %get-tuple-element.177), channel_id=1, source_target_pairs={{0,8},{4,12},{8,0},{12,4},{16,24},{20,28},{24,16},{28,20},{1,9},{5... | collective-permute-start | bytes 245768 | tf_op jit(solution)/shard_map/ppermute | solution.py:1037
  402.4 5.3 %collective-permute-done.36 = bf16[64,640]{1,0:T(8,128)(2,1)S(1)} collective-permute-done((bf16[64,640]{1,0:T(8,128)(2,1)S(1)}, bf16[64,640]{1,0:T(8,128)(2,1)S(1)}, u32[]{:S(2)}, u32[]{:S(2)}) %collective-permute-start.36) | collective-permute-done | bytes 81952 | tf_op jit(solution)/shard_map/ppermute | solution.py:1037
  (219 shorter events, 120.3 us)
Async XLA Ops:
  25.0 20.4 %collective-permute-start.18 = (bf16[192,640]{1,0:T(8,128)(2,1)S(1)}, bf16[192,640]{1,0:T(8,128)(2,1)S(1)}, u32[]{:S(2)}, u32[]{:S(2)}) collective-permute-start(bf16[192,640]{1,0:T(8,128)(2,1)S(1)} %get-tuple-element.59), channel_id=1, source_target_pairs={{0,16},{4,20},{8,24},{12,28},{16,0},{20,4},{24,8},{28,12},{1,17},{... | collective-permute-start | bytes 737288 | tf_op jit(solution)/shard_map/ppermute | solution.py:1037
  37.8 28.9 %collective-permute-start.12 = (bf16[8,64,640]{2,1,0:T(8,128)(2,1)}, bf16[8,64,640]{2,1,0:T(8,128)(2,1)S(1)}, u32[]{:S(2)}, u32[]{:S(2)}) collective-permute-start(bf16[8,64,640]{2,1,0:T(8,128)(2,1)} %constant_dynamic-update-slice_fusion.5.b0), channel_id=1, source_target_pairs={{0,4},{4,0},{8,12},{12,8},{16,20},{20,16},{24,28},{28,24},{1,5},{5... | collective-permute-start | bytes 1966088 | tf_op jit(solution)/shard_map/ppermute | solution.py:1037
  40.0 27.5 %collective-permute-start.5 = (bf16[8,64,640]{2,1,0:T(8,128)(2,1)}, bf16[8,64,640]{2,1,0:T(8,128)(2,1)S(1)}, u32[]{:S(2)}, u32[]{:S(2)}) collective-permute-start(bf16[8,64,640]{2,1,0:T(8,128)(2,1)} %constant_dynamic-update-slice_fusion.a0), channel_id=1, source_target_pairs={{0,2},{1,3},{2,0},{3,1},{4,6},{5,7},{6,4},{7,5},{8,10},{9,11},{10,... | collective-permute-start | bytes 1966088 | tf_op jit(solution)/shard_map/ppermute | solution.py:1037
  45.5 21.1 %collective-permute-start.15 = (bf16[192,640]{1,0:T(8,128)(2,1)S(1)}, bf16[192,640]{1,0:T(8,128)(2,1)S(1)}, u32[]{:S(2)}, u32[]{:S(2)}) collective-permute-start(bf16[192,640]{1,0:T(8,128)(2,1)S(1)} %get-tuple-element.58), channel_id=1, source_target_pairs={{0,16},{4,20},{8,24},{12,28},{16,0},{20,4},{24,8},{28,12},{1,17},{... | collective-permute-start | bytes 737288 | tf_op jit(solution)/shard_map/ppermute | solution.py:1037
  68.4 19.5 %collective-permute-start.21 = (bf16[4,192,640]{2,1,0:T(8,128)(2,1)S(1)}, bf16[4,192,640]{2,1,0:T(8,128)(2,1)}, u32[]{:S(2)}, u32[]{:S(2)}) collective-permute-start(bf16[4,192,640]{2,1,0:T(8,128)(2,1)S(1)} %pad_maximum_fusion.1), channel_id=1, source_target_pairs={{0,2},{1,3},{2,0},{3,1},{4,6},{5,7},{6,4},{7,5},{8,10},{9,11},{10,... | collective-permute-start | bytes 2949128 | tf_op jit(solution)/shard_map/ppermute | solution.py:1037
  72.7 22.9 %collective-permute-start.20 = (bf16[4,192,640]{2,1,0:T(8,128)(2,1)S(1)}, bf16[4,192,640]{2,1,0:T(8,128)(2,1)S(1)}, u32[]{:S(2)}, u32[]{:S(2)}) collective-permute-start(bf16[4,192,640]{2,1,0:T(8,128)(2,1)S(1)} %pad_maximum_fusion), channel_id=1, source_target_pairs={{0,4},{4,0},{8,12},{12,8},{16,20},{20,16},{24,28},{28,24},{1,5},{5... | collective-permute-start | bytes 2949128 | tf_op jit(solution)/shard_map/ppermute | solution.py:1037
  90.3 43.7 %collective-permute-start.26 = (bf16[8,192,640]{2,1,0:T(8,128)(2,1)}, bf16[8,192,640]{2,1,0:T(8,128)(2,1)}, u32[]{:S(2)}, u32[]{:S(2)}) collective-permute-start(bf16[8,192,640]{2,1,0:T(8,128)(2,1)} %constant_dynamic-update-slice_fusion.12.u0), channel_id=1, source_target_pairs={{0,4},{4,0},{8,12},{12,8},{16,20},{20,16},{24,28},{28,24},{1,5},{5... | collective-permute-start | bytes 5898248 | tf_op jit(solution)/shard_map/ppermute | solution.py:1037
  96.7 37.4 %collective-permute-start.23 = (bf16[8,192,640]{2,1,0:T(8,128)(2,1)}, bf16[8,192,640]{2,1,0:T(8,128)(2,1)}, u32[]{:S(2)}, u32[]{:S(2)}) collective-permute-start(bf16[8,192,640]{2,1,0:T(8,128)(2,1)} %constant_dynamic-update-slice_fusion.10.g0), channel_id=1, source_target_pairs={{0,2},{1,3},{2,0},{3,1},{4,6},{5,7},{6,4},{7,5},{8,10},{9,11},{10,... | collective-permute-start | bytes 5898248 | tf_op jit(solution)/shard_map/ppermute | solution.py:1037
  113.5 56.2 %collective-permute-start.25 = (bf16[8,192,640]{2,1,0:T(8,128)(2,1)}, bf16[8,192,640]{2,1,0:T(8,128)(2,1)S(1)}, u32[]{:S(2)}, u32[]{:S(2)}) collective-permute-start(bf16[8,192,640]{2,1,0:T(8,128)(2,1)} %constant_dynamic-update-slice_fusion.12.u0), channel_id=1, source_target_pairs={{0,1},{1,0},{2,3},{3,2},{4,5},{5,4},{6,7},{7,6},{8,9},{9,8},{10,11... | collective-permute-start | bytes 5898248 | tf_op jit(solution)/shard_map/ppermute | solution.py:1037
  113.6 56.1 %collective-permute-start.22 = (bf16[8,192,640]{2,1,0:T(8,128)(2,1)}, bf16[8,192,640]{2,1,0:T(8,128)(2,1)S(1)}, u32[]{:S(2)}, u32[]{:S(2)}) collective-permute-start(bf16[8,192,640]{2,1,0:T(8,128)(2,1)} %constant_dynamic-update-slice_fusion.10.g0), channel_id=1, source_target_pairs={{0,1},{1,0},{2,3},{3,2},{4,5},{5,4},{6,7},{7,6},{8,9},{9,8},{10,11... | collective-permute-start | bytes 5898248 | tf_op jit(solution)/shard_map/ppermute | solution.py:1037
  134.0 35.7 %collective-permute-start.27 = (bf16[8,192,640]{2,1,0:T(8,128)(2,1)}, bf16[8,192,640]{2,1,0:T(8,128)(2,1)}, u32[]{:S(2)}, u32[]{:S(2)}) collective-permute-start(bf16[8,192,640]{2,1,0:T(8,128)(2,1)} %collective-permute-done.26.u2), channel_id=1, source_target_pairs={{0,1},{1,0},{2,3},{3,2},{4,5},{5,4},{6,7},{7,6},{8,9},{9,8},{10,11... | collective-permute-start | bytes 5898248 | tf_op jit(solution)/shard_map/ppermute | solution.py:1037
  134.1 35.7 %collective-permute-start.24 = (bf16[8,192,640]{2,1,0:T(8,128)(2,1)}, bf16[8,192,640]{2,1,0:T(8,128)(2,1)}, u32[]{:S(2)}, u32[]{:S(2)}) collective-permute-start(bf16[8,192,640]{2,1,0:T(8,128)(2,1)} %collective-permute-done.23.g2), channel_id=1, source_target_pairs={{0,1},{1,0},{2,3},{3,2},{4,5},{5,4},{6,7},{7,6},{8,9},{9,8},{10,11... | collective-permute-start | bytes 5898248 | tf_op jit(solution)/shard_map/ppermute | solution.py:1037
  220.9 25.0 %collective-permute-start.29 = (bf16[2,8,192,640]{3,2,1,0:T(8,128)(2,1)}, bf16[2,8,192,640]{3,2,1,0:T(8,128)(2,1)}, u32[]{:S(2)}, u32[]{:S(2)}) collective-permute-start(bf16[2,8,192,640]{3,2,1,0:T(8,128)(2,1)} %get-tuple-element.84), channel_id=1, source_target_pairs={{0,1},{1,0},{2,3},{3,2},{4,5},{5,4},{6,7},{7,6},{8,9},{9,8},{10,11... | collective-permute-start | bytes 11796488 | tf_op jit(solution)/shard_map/ppermute | solution.py:1037
  221.0 32.3 %collective-permute-start.28 = (bf16[2,8,192,640]{3,2,1,0:T(8,128)(2,1)}, bf16[2,8,192,640]{3,2,1,0:T(8,128)(2,1)}, u32[]{:S(2)}, u32[]{:S(2)}) collective-permute-start(bf16[2,8,192,640]{3,2,1,0:T(8,128)(2,1)} %get-tuple-element.83), channel_id=1, source_target_pairs={{0,1},{1,0},{2,3},{3,2},{4,5},{5,4},{6,7},{7,6},{8,9},{9,8},{10,11... | collective-permute-start | bytes 11796488 | tf_op jit(solution)/shard_map/ppermute | solution.py:1037
  251.8 48.2 %collective-permute-start.31 = (bf16[8,192,640]{2,1,0:T(8,128)(2,1)}, bf16[8,192,640]{2,1,0:T(8,128)(2,1)}, u32[]{:S(2)}, u32[]{:S(2)}) collective-permute-start(bf16[8,192,640]{2,1,0:T(8,128)(2,1)} %get-tuple-element.156), channel_id=1, source_target_pairs={{0,4},{4,0},{8,12},{12,8},{16,20},{20,16},{24,28},{28,24},{1,5},{5... | collective-permute-start | bytes 5898248 | tf_op jit(solution)/shard_map/ppermute | solution.py:1037
  257.9 46.8 %collective-permute-start.30 = (bf16[8,192,640]{2,1,0:T(8,128)(2,1)}, bf16[8,192,640]{2,1,0:T(8,128)(2,1)}, u32[]{:S(2)}, u32[]{:S(2)}) collective-permute-start(bf16[8,192,640]{2,1,0:T(8,128)(2,1)} %get-tuple-element.158), channel_id=1, source_target_pairs={{0,2},{1,3},{2,0},{3,1},{4,6},{5,7},{6,4},{7,5},{8,10},{9,11},{10,... | collective-permute-start | bytes 5898248 | tf_op jit(solution)/shard_map/ppermute | solution.py:1037
  303.2 24.0 %collective-permute-start.48 = (bf16[4,192,640]{2,1,0:T(8,128)(2,1)}, bf16[4,192,640]{2,1,0:T(8,128)(2,1)S(1)}, u32[]{:S(2)}, u32[]{:S(2)}) collective-permute-start(bf16[4,192,640]{2,1,0:T(8,128)(2,1)} %get-tuple-element.160), channel_id=1, source_target_pairs={{0,2},{1,3},{2,0},{3,1},{4,6},{5,7},{6,4},{7,5},{8,10},{9,11},{10,... | collective-permute-start | bytes 2949128 | tf_op jit(solution)/shard_map/ppermute | solution.py:1037
  318.1 28.1 %collective-permute-start.38 = (bf16[2,8,64,640]{3,2,1,0:T(8,128)(2,1)}, bf16[2,8,64,640]{3,2,1,0:T(8,128)(2,1)}, u32[]{:S(2)}, u32[]{:S(2)}) collective-permute-start(bf16[2,8,64,640]{3,2,1,0:T(8,128)(2,1)} %get-tuple-element.104), channel_id=1, source_target_pairs={{0,1},{1,0},{2,3},{3,2},{4,5},{5,4},{6,7},{7,6},{8,9},{9,8},{10,11... | collective-permute-start | bytes 3932168 | tf_op jit(solution)/shard_map/ppermute | solution.py:1037
  318.1 24.5 %collective-permute-start.44 = (bf16[4,192,640]{2,1,0:T(8,128)(2,1)}, bf16[4,192,640]{2,1,0:T(8,128)(2,1)}, u32[]{:S(2)}, u32[]{:S(2)}) collective-permute-start(bf16[4,192,640]{2,1,0:T(8,128)(2,1)} %get-tuple-element.162), channel_id=1, source_target_pairs={{0,4},{4,0},{8,12},{12,8},{16,20},{20,16},{24,28},{28,24},{1,5},{5... | collective-permute-start | bytes 2949128 | tf_op jit(solution)/shard_map/ppermute | solution.py:1037
  318.6 34.4 %collective-permute-start.32 = (bf16[2,8,64,640]{3,2,1,0:T(8,128)(2,1)}, bf16[2,8,64,640]{3,2,1,0:T(8,128)(2,1)}, u32[]{:S(2)}, u32[]{:S(2)}) collective-permute-start(bf16[2,8,64,640]{3,2,1,0:T(8,128)(2,1)} %get-tuple-element.102), channel_id=1, source_target_pairs={{0,1},{1,0},{2,3},{3,2},{4,5},{5,4},{6,7},{7,6},{8,9},{9,8},{10,11... | collective-permute-start | bytes 3932168 | tf_op jit(solution)/shard_map/ppermute | solution.py:1037
  327.4 27.6 %collective-permute-start.49 = (bf16[192,640]{1,0:T(8,128)(2,1)S(1)}, bf16[192,640]{1,0:T(8,128)(2,1)S(1)}, u32[]{:S(2)}, u32[]{:S(2)}) collective-permute-start(bf16[192,640]{1,0:T(8,128)(2,1)S(1)} %get-tuple-element.167), channel_id=1, source_target_pairs={{0,8},{4,12},{8,0},{12,4},{16,24},{20,28},{24,16},{28,20},{1,9},{5... | collective-permute-start | bytes 737288 | tf_op jit(solution)/shard_map/ppermute | solution.py:1037
  333.5 23.8 %collective-permute-start.50 = (bf16[192,640]{1,0:T(8,128)(2,1)S(1)}, bf16[192,640]{1,0:T(8,128)(2,1)S(1)}, u32[]{:S(2)}, u32[]{:S(2)}) collective-permute-start(bf16[192,640]{1,0:T(8,128)(2,1)S(1)} %get-tuple-element.169), channel_id=1, source_target_pairs={{0,16},{4,20},{8,24},{12,28},{16,0},{20,4},{24,8},{28,12},{1,17},{... | collective-permute-start | bytes 737288 | tf_op jit(solution)/shard_map/ppermute | solution.py:1037
  353.1 21.2 %collective-permute-start.46 = (bf16[192,640]{1,0:T(8,128)(2,1)S(1)}, bf16[192,640]{1,0:T(8,128)(2,1)S(1)}, u32[]{:S(2)}, u32[]{:S(2)}) collective-permute-start(bf16[192,640]{1,0:T(8,128)(2,1)S(1)} %get-tuple-element.172), channel_id=1, source_target_pairs={{0,16},{4,20},{8,24},{12,28},{16,0},{20,4},{24,8},{28,12},{1,17},{... | collective-permute-start | bytes 737288 | tf_op jit(solution)/shard_map/ppermute | solution.py:1037
  357.9 20.8 %collective-permute-start.33 = (bf16[8,64,640]{2,1,0:T(8,128)(2,1)S(1)}, bf16[8,64,640]{2,1,0:T(8,128)(2,1)S(1)}, u32[]{:S(2)}, u32[]{:S(2)}) collective-permute-start(bf16[8,64,640]{2,1,0:T(8,128)(2,1)S(1)} %get-tuple-element.166), channel_id=1, source_target_pairs={{0,4},{4,0},{8,12},{12,8},{16,20},{20,16},{24,28},{28,24},{1,5},{5... | collective-permute-start | bytes 1966088 | tf_op jit(solution)/shard_map/ppermute | solution.py:1037
  (54 other events, 598.8 us)
